TPU v7x, 32 devices: a whole 2x2x4 slice. The times are simulated.
32 devices in a mesh: dp: 2 (over core), context: 4 (over y, x), expert: 4 (over z).
Axes of the slice: x: 2, y: 2, z: 4, core: 2. Of those that a mesh axis runs over, the one named last changes fastest.
Arguments:
- layer_input: bfloat16 [2, 2048, 2048], P('dp', ('context', 'expert')), may hold values from -6 to 6
- grad_output: bfloat16 [2, 2048, 2048], P('dp', ('context', 'expert')), may hold values from -6 to 6
- attn_gain: float32 [2048], replicated, may hold values from 0.5 to 1.5
- query_weight: bfloat16 [2048, 4096], P(None, 'expert'), may hold values from -0.125 to 0.125
- key_weight: bfloat16 [2048, 512], P(None, 'expert'), may hold values from -0.125 to 0.125
- value_weight: bfloat16 [2048, 512], P(None, 'expert'), may hold values from -0.125 to 0.125
- q_gain: float32 [128], replicated, may hold values from 0.25 to 1.75
- k_gain: float32 [128], replicated, may hold values from 0.25 to 1.75
- output_weight: bfloat16 [4096, 2048], P('expert'), may hold values from -1.75 to 1.75
- mlp_gain: float32 [2048], replicated, may hold values from 0.5 to 1.5
- router: bfloat16 [2048, 32], replicated, may hold values from -0.0625 to 0.0625
- w_gate: bfloat16 [32, 2048, 768], P(('dp', 'context', 'expert')), may hold values from -0.125 to 0.125
- w_up: bfloat16 [32, 2048, 768], P(('dp', 'context', 'expert')), may hold values from -0.125 to 0.125
- w_down: bfloat16 [32, 768, 2048], P(('dp', 'context', 'expert')), may hold values from -0.875 to 0.875
- routes: int32 [2, 2048, 8], P('dp', ('context', 'expert')), may hold values from 0 to 31, all different within a row; in each aligned block of 128 rows (0 to 127, 128 to 255, ..., all dimensions but the last counted through in order) at most 36 rows name the same one
- half_order: int32 [8], replicated, may hold values from 0 to 7, each once
Outputs:
- layer_output: bfloat16 [2, 2048, 2048], P('dp', ('context', 'expert'))
- grad_input: float32 [2, 2048, 2048], P('dp', ('context', 'expert'))
- grad_attn_gain: float32 [2048], replicated
- grad_w_query: float32 [2048, 4096], P(None, 'expert')
- grad_w_key: float32 [2048, 512], P(None, 'expert')
- grad_w_value: float32 [2048, 512], P(None, 'expert')
- grad_q_gain: float32 [128], replicated
- grad_k_gain: float32 [128], replicated
- grad_w_out: float32 [4096, 2048], P('expert')
- grad_mlp_gain: float32 [2048], replicated
- grad_router: float32 [2048, 32], replicated
- grad_w_gate: float32 [32, 2048, 768], P(('dp', 'context', 'expert'))
- grad_w_up: float32 [32, 2048, 768], P(('dp', 'context', 'expert'))
- grad_w_down: float32 [32, 768, 2048], P(('dp', 'context', 'expert'))
Inputs may be any that keep to these rules, and one draw needn't show every extreme that they name: `routes`: each token names 8 different experts. In each aligned block of 128 tokens (the tokens of one device) no expert is named by more than 36 of them, a bound that some block reaches. `half_order`: each half-block appears once.
All inputs are finite; a program needn't handle non-finite values.
Results may differ from a plain program's by a relative error of at most 0.02.
Values may be sent and summed in bfloat16 or wider, within the bound.
No kernel may reach another device: no remote copies, remote signals or barrier semaphores. Data moves between devices by JAX's collectives and lax.ppermute only.
A program may use at most 320 MiB of HBM per device.

v0:
```python
import functools
import math

import jax
import jax.numpy as jnp
from jax import lax
from jax.experimental import pallas as pl
from jax.experimental.pallas import tpu as pltpu
from jax.sharding import PartitionSpec as P

EPS = 1e-06
THETA = 1000000.0
TILE = 256
PIECE = 128
VMEM_BYTES = 56 * 1024 * 1024
LOG2E = math.log2(math.e)
LOW = jnp.bfloat16
F32 = jnp.float32
ALL_AXES = ("dp", "context", "expert")
GROUP_AXES = ("dp", "context")


def dot_nn(a, b):
    return lax.dot_general(a, b, (((1,), (0,)), ((), ())), preferred_element_type=F32)


def dot_nt(a, b):
    return lax.dot_general(a, b, (((1,), (1,)), ((), ())), preferred_element_type=F32)


def dot_tn(a, b):
    return lax.dot_general(a, b, (((0,), (0,)), ((), ())), preferred_element_type=F32)


def params(**more):
    return pltpu.CompilerParams(vmem_limit_bytes=VMEM_BYTES, **more)


def cost(flops, nbytes, exps=0):
    return pl.CostEstimate(flops=int(flops), bytes_accessed=int(nbytes), transcendentals=int(exps))


def head_forward(u, gain, cos2, sin2):
    rr = lax.rsqrt(jnp.mean(u * u, axis=-1, keepdims=True) + EPS)
    y = u * rr * gain
    return y * cos2 + pltpu.roll(y, 64, 1) * sin2


def head_backward(gy, u, gain, cos2, sin2):
    g = gy * cos2 - pltpu.roll(gy, 64, 1) * sin2
    rr = lax.rsqrt(jnp.mean(u * u, axis=-1, keepdims=True) + EPS)
    n = u * rr
    gn = g * gain
    grad = rr * (gn - n * jnp.mean(gn * n, axis=-1, keepdims=True))
    return grad, jnp.sum(g * n, axis=0, keepdims=True)


def query_kernel(x_ref, w_ref, gain_ref, cos_ref, sin_ref, rot_ref, proj_ref):
    tiles, heads, rows, size = rot_ref.shape
    acc = dot_nn(x_ref[...], w_ref[...])
    for h in range(heads):
        u = acc[:, h * size : (h + 1) * size]
        rot = head_forward(u, gain_ref[...], cos_ref[...], sin_ref[...])
        proj_ref[:, h] = u.reshape(tiles, rows, size)
        rot_ref[:, h] = rot.astype(LOW).reshape(tiles, rows, size)


def project_queries(normed, weight, gain, cos2, sin2):
    block, width = normed.shape
    size = cos2.shape[1]
    heads = weight.shape[1] // size
    tiles = block // TILE
    whole = lambda i: (0, 0)
    per = lambda i: (0, i, 0, 0)
    shape = (tiles, heads, TILE, size)
    return pl.pallas_call(
        query_kernel,
        grid=(heads // 2,),
        in_specs=[
            pl.BlockSpec((block, width), whole),
            pl.BlockSpec((width, 2 * size), lambda i: (0, i)),
            pl.BlockSpec((1, size), whole),
            pl.BlockSpec((block, size), whole),
            pl.BlockSpec((block, size), whole),
        ],
        out_specs=[pl.BlockSpec((tiles, 2, TILE, size), per)] * 2,
        out_shape=[jax.ShapeDtypeStruct(shape, LOW), jax.ShapeDtypeStruct(shape, F32)],
        compiler_params=params(),
        cost_estimate=cost(2 * block * width * heads * size, 12e6),
    )(normed, weight, gain[None], cos2, sin2)


def put_in_order(place, refs, out_ref):
    n = (len(refs) + 1) // 2
    rows = refs[0].shape[0]
    for distance in range(1 - n, n):
        ref = refs[distance + n - 1]
        at = place + distance

        @pl.when(jnp.logical_and(at >= 0, at < n))
        def _():
            out_ref[pl.ds(pl.multiple_of(at * rows, rows), rows), :] = ref[...]


def chunk_list(found):
    n = (len(found) + 1) // 2
    return [found[distance] for distance in range(1 - n, n)]


def key_kernel(factor, n_chunks, place_ref, *refs):
    w_ref, gain_ref, cos_ref, sin_ref, g_ref, mask_ref = refs[n_chunks:-4]
    rows_ref, kv_ref, proj_ref, wide_ref = refs[-4:]
    size = proj_ref.shape[1]
    width = g_ref.shape[1]
    put_in_order(place_ref[0], refs[:n_chunks], rows_ref)
    wide_ref[:, :width] = g_ref[...]
    wide_ref[:, width:] = mask_ref[...].astype(LOW)
    acc = dot_nn(rows_ref[...], w_ref[...])
    u = acc[:, :size]
    rot = head_forward(u, gain_ref[...], cos_ref[...], sin_ref[...])
    proj_ref[...] = u
    kv_ref[:, :size] = (rot * factor).astype(LOW)
    kv_ref[:, size:] = acc[:, size:].astype(LOW)


def full(shape):
    return pl.BlockSpec(shape, lambda *_: (0,) * len(shape))


def project_keys(place, found, weight, gain, cos2, sin2, factor, g, mask):
    chunks = chunk_list(found)
    rows, width = chunks[0].shape
    block, size = cos2.shape
    operands = [*chunks, weight, gain[None], cos2, sin2, g, mask]
    shapes = [
        jax.ShapeDtypeStruct((block, width), LOW),
        jax.ShapeDtypeStruct((block, 2 * size), LOW),
        jax.ShapeDtypeStruct((block, size), F32),
        jax.ShapeDtypeStruct((rows, width + mask.shape[1]), LOW),
    ]
    return pl.pallas_call(
        functools.partial(key_kernel, factor, len(chunks)),
        grid_spec=pltpu.PrefetchScalarGridSpec(
            num_scalar_prefetch=1,
            grid=(1,),
            in_specs=[full(x.shape) for x in operands],
            out_specs=[full(x.shape) for x in shapes],
        ),
        out_shape=shapes,
        compiler_params=params(),
        cost_estimate=cost(4 * block * width * size, 8e6),
    )(place, *operands)


def in_order(last, step):
    lax.fori_loop(0, lax.div(last, 2), lambda p, c: (step([2 * p, 2 * p + 1], False), c)[1], 0)

    @pl.when(lax.rem(last, 2) == 1)
    def _():
        step([last - 1, last], True)

    @pl.when(lax.rem(last, 2) == 0)
    def _():
        step([last], True)


def attend_kernel(qpos_ref, kidx_ref, q_ref, kv_ref, *rest):
    out_ref, inv_ref, acc_ref = rest[-3:]
    heads, rows, size = q_ref.shape[1:]
    acc_ref[...] = jnp.zeros_like(acc_ref)

    def step(places, masked):
        starts = [pl.multiple_of(kidx_ref[place] * rows, rows) for place in places]
        count = len(places) * rows
        keys = jnp.concatenate([kv_ref[pl.ds(start, rows), :size] for start in starts], axis=0)
        values = jnp.concatenate([kv_ref[pl.ds(start, rows), size:] for start in starts], axis=0)
        values = jnp.concatenate([values, jnp.ones((count, size), LOW)], axis=1)
        for h in range(heads):
            for first in range(0, rows, PIECE):
                part = slice(first, first + PIECE)
                e = jnp.exp2(dot_nt(q_ref[0, h, part], keys))
                if masked:
                    qi = lax.broadcasted_iota(jnp.int32, e.shape, 0) + first
                    ki = lax.broadcasted_iota(jnp.int32, e.shape, 1) - (count - rows)
                    e = jnp.where(ki <= qi, e, 0.0)
                acc_ref[h, part] += dot_nn(e.astype(LOW), values)

    in_order(qpos_ref[pl.program_id(0)], step)
    for h in range(heads):
        inv = 1.0 / acc_ref[h, :, size:]
        inv_ref[0, h] = inv
        out_ref[:, h * size : (h + 1) * size] = (acc_ref[h, :, :size] * inv).astype(LOW)


def attend(qpos, kidx, queries, kv, others):
    tiles, heads, rows, size = queries.shape
    seq = kv.shape[0]
    return pl.pallas_call(
        attend_kernel,
        grid_spec=pltpu.PrefetchScalarGridSpec(
            num_scalar_prefetch=2,
            grid=(tiles,),
            in_specs=[
                pl.BlockSpec((1, heads, rows, size), lambda i, a, b: (i, 0, 0, 0)),
                pl.BlockSpec((seq, 2 * size), lambda i, a, b: (0, 0)),
            ]
            + [pl.BlockSpec(memory_space=pl.ANY)] * len(others),
            out_specs=[
                pl.BlockSpec((rows, heads * size), lambda i, a, b: (i, 0)),
                pl.BlockSpec((1, heads, rows, size), lambda i, a, b: (i, 0, 0, 0)),
            ],
            scratch_shapes=[pltpu.VMEM((heads, rows, 2 * size), F32)],
        ),
        out_shape=[
            jax.ShapeDtypeStruct((tiles * rows, heads * size), LOW),
            jax.ShapeDtypeStruct((tiles, heads, rows, size), F32),
        ],
        compiler_params=params(),
        cost_estimate=cost(
            6 * tiles * rows * heads * seq * size, 8e6, tiles * rows * heads * seq
        ),
    )(qpos, kidx, queries, kv, *others)


def grad_out_kernel(rows_ref, w_ref, o_ref, inv_ref, *rest):
    do_ref, centre_ref = rest[-2:]
    tiles, heads, rows, size = do_ref.shape
    acc = dot_nt(rows_ref[...], w_ref[...])
    for t in range(tiles):
        for h in range(heads):
            part = slice(t * rows, (t + 1) * rows), slice(h * size, (h + 1) * size)
            low = (acc[part] * inv_ref[t, h]).astype(LOW)
            do_ref[t, h] = low
            product = low.astype(F32) * o_ref[part].astype(F32)
            centre = jnp.sum(jnp.transpose(product), axis=0, keepdims=True)
            centre_ref[t, h] = jnp.broadcast_to(centre, (8, rows))


def grad_attended(grad_rows, weight, attended, inverse, others):
    tiles, heads, rows, size = inverse.shape
    block, width = grad_rows.shape
    return pl.pallas_call(
        grad_out_kernel,
        grid=(heads // 2,),
        in_specs=[
            pl.BlockSpec((block, width), lambda i: (0, 0)),
            pl.BlockSpec((2 * size, width), lambda i: (i, 0)),
            pl.BlockSpec((block, 2 * size), lambda i: (0, i)),
            pl.BlockSpec((tiles, 2, rows, size), lambda i: (0, i, 0, 0)),
        ]
        + [pl.BlockSpec(memory_space=pl.ANY)] * len(others),
        out_specs=[
            pl.BlockSpec((tiles, 2, rows, size), lambda i: (0, i, 0, 0)),
            pl.BlockSpec((tiles, 2, 8, rows), lambda i: (0, i, 0, 0)),
        ],
        out_shape=[
            jax.ShapeDtypeStruct((tiles, heads, rows, size), LOW),
            jax.ShapeDtypeStruct((tiles, heads, 8, rows), F32),
        ],
        compiler_params=params(),
        cost_estimate=cost(2 * block * width * heads * size, 12e6),
    )(grad_rows, weight, attended, inverse, *others)


def attend_back_kernel(
    qpos_ref,
    kidx_ref,
    q_ref,
    do_ref,
    centre_ref,
    kv_ref,
    kt_ref,
    proj_ref,
    gain_ref,
    cos_ref,
    sin_ref,
    *rest,
):
    dkv_ref, dq_ref, dgain_ref, acc_ref, e_ref, ds_ref = rest[-6:]
    heads, rows, size = q_ref.shape[1:]

    @pl.when(pl.program_id(0) == 0)
    def _():
        dkv_ref[...] = jnp.zeros_like(dkv_ref)
        dgain_ref[...] = jnp.zeros_like(dgain_ref)

    acc_ref[...] = jnp.zeros_like(acc_ref)

    def step(places, masked):
        starts = [pl.multiple_of(kidx_ref[place] * rows, rows) for place in places]
        count = len(places) * rows
        keys = jnp.concatenate([kv_ref[pl.ds(start, rows), :size] for start in starts], axis=0)
        values = jnp.concatenate([kv_ref[pl.ds(start, rows), size:] for start in starts], axis=0)
        keys_t = jnp.concatenate([kt_ref[:, pl.ds(start, rows)] for start in starts], axis=1)
        for h in range(heads):
            query, grad = q_ref[0, h], do_ref[0, h]
            centre = centre_ref[0, h, 0:1]
            columns = slice(h * rows, (h + 1) * rows)
            for first in range(0, count, PIECE):
                part = slice(first, first + PIECE)
                e = jnp.exp2(dot_nt(keys[part], query))
                if masked and first >= count - rows:
                    ki = lax.broadcasted_iota(jnp.int32, e.shape, 0) + (first - (count - rows))
                    qi = lax.broadcasted_iota(jnp.int32, e.shape, 1)
                    e = jnp.where(ki <= qi, e, 0.0)
                ds = e * (dot_nt(values[part], grad) - centre)
                e_ref[part, columns] = e.astype(LOW)
                ds_ref[part, columns] = ds.astype(LOW)
            acc_ref[h] += dot_nn(keys_t, ds_ref[:count, columns])
        dk = dot_nn(ds_ref[:count], q_ref[0].reshape(heads * rows, size))
        dv = dot_nn(e_ref[:count], do_ref[0].reshape(heads * rows, size))
        for k, start in enumerate(starts):
            dkv_ref[pl.ds(start, rows), :size] += dk[k * rows : (k + 1) * rows]
            dkv_ref[pl.ds(start, rows), size:] += dv[k * rows : (k + 1) * rows]

    in_order(qpos_ref[pl.program_id(0)], step)
    total = jnp.zeros((1, size), F32)
    for h in range(heads):
        grad, gain_part = head_backward(
            jnp.transpose(acc_ref[h]) * (1.0 / LOG2E),
            proj_ref[0, h],
            gain_ref[...],
            cos_ref[...],
            sin_ref[...],
        )
        dq_ref[:, h * size : (h + 1) * size] = grad.astype(LOW)
        total += gain_part
    dgain_ref[...] += total


def attend_back(qpos, kidx, queries, grads, centre, kv, keys_t, proj, gain, cos2, sin2, others):
    tiles, heads, rows, size = queries.shape
    seq = kv.shape[0]
    per = pl.BlockSpec((1, heads, rows, size), lambda i, a, b: (i, 0, 0, 0))
    flat = lambda i, a, b: (0, 0)
    rowwise = lambda i, a, b: (i, 0)
    return pl.pallas_call(
        attend_back_kernel,
        grid_spec=pltpu.PrefetchScalarGridSpec(
            num_scalar_prefetch=2,
            grid=(tiles,),
            in_specs=[
                per,
                per,
                pl.BlockSpec((1, heads, 8, rows), lambda i, a, b: (i, 0, 0, 0)),
                pl.BlockSpec((seq, 2 * size), flat),
                pl.BlockSpec((size, seq), flat),
                per,
                pl.BlockSpec((1, size), flat),
                pl.BlockSpec((rows, size), rowwise),
                pl.BlockSpec((rows, size), rowwise),
            ]
            + [pl.BlockSpec(memory_space=pl.ANY)] * len(others),
            out_specs=[
                pl.BlockSpec((seq, 2 * size), flat),
                pl.BlockSpec((rows, heads * size), rowwise),
                pl.BlockSpec((1, size), flat),
            ],
            scratch_shapes=[pltpu.VMEM((heads, size, rows), F32)]
            + [pltpu.VMEM((2 * rows, heads * rows), LOW)] * 2,
        ),
        out_shape=[
            jax.ShapeDtypeStruct((seq, 2 * size), F32),
            jax.ShapeDtypeStruct((tiles * rows, heads * size), LOW),
            jax.ShapeDtypeStruct((1, size), F32),
        ],
        compiler_params=params(),
        cost_estimate=cost(
            15 * tiles * rows * heads * seq * size, 12e6, tiles * rows * heads * seq
        ),
    )(qpos, kidx, queries, grads, centre, kv, keys_t, proj, gain[None], cos2, sin2, *others)


def out_kernel(a_ref, b_ref, *rest):
    rest[-1][...] = dot_nn(a_ref[...], b_ref[...]).astype(LOW)


def out_dot(a, b, others):
    block, inner = a.shape
    columns = b.shape[1]
    tile = min(columns, 512)
    return pl.pallas_call(
        out_kernel,
        grid=(columns // tile,),
        in_specs=[
            pl.BlockSpec((block, inner), lambda i: (0, 0)),
            pl.BlockSpec((inner, tile), lambda i: (0, i)),
        ]
        + [pl.BlockSpec(memory_space=pl.ANY)] * len(others),
        out_specs=pl.BlockSpec((block, tile), lambda i: (0, i)),
        out_shape=jax.ShapeDtypeStruct((block, columns), LOW),
        compiler_params=params(),
        cost_estimate=cost(2 * block * inner * columns, 8e6),
    )(a, b, *others)


def token_kernel(a_ref, b_ref, *rest):
    rest[-1][...] = dot_tn(a_ref[...], b_ref[...]).astype(LOW)


def token_dot(a, b, others):
    block, rows = a.shape
    columns = b.shape[1]
    tile = min(rows, 512)
    return pl.pallas_call(
        token_kernel,
        grid=(rows // tile,),
        in_specs=[
            pl.BlockSpec((block, tile), lambda i: (0, i)),
            pl.BlockSpec((block, columns), lambda i: (0, 0)),
        ]
        + [pl.BlockSpec(memory_space=pl.ANY)] * len(others),
        out_specs=pl.BlockSpec((tile, columns), lambda i: (i, 0)),
        out_shape=jax.ShapeDtypeStruct((rows, columns), LOW),
        compiler_params=params(),
        cost_estimate=cost(2 * block * rows * columns, 6e6),
    )(a, b, *others)


def halves_kernel(d_ref, a_ref, b_ref, *rest):
    send_ref, keep_ref = rest[-2:]
    product = dot_tn(a_ref[...], b_ref[...]).astype(LOW)

    @pl.when(pl.program_id(0) == 0)
    def _():
        send_ref[...] = product

    @pl.when(pl.program_id(0) == 1)
    def _():
        keep_ref[...] = product


def token_halves(a, b, others):
    block, rows = a.shape
    columns = b.shape[1]
    tiles = 2 if rows % 512 == 0 else 1
    tile = rows // (2 * tiles)
    d = lax.axis_index("dp").astype(jnp.int32)[None]
    half = jax.ShapeDtypeStruct((rows // 2, columns), LOW)
    return pl.pallas_call(
        halves_kernel,
        grid_spec=pltpu.PrefetchScalarGridSpec(
            num_scalar_prefetch=1,
            grid=(2, tiles),
            in_specs=[
                pl.BlockSpec(
                    (block, tile),
                    lambda h, j, d: (0, ((1 - d[0]) * (1 - h) + d[0] * h) * tiles + j),
                ),
                pl.BlockSpec((block, columns), lambda h, j, d: (0, 0)),
            ]
            + [pl.BlockSpec(memory_space=pl.ANY)] * len(others),
            out_specs=[
                pl.BlockSpec((tile, columns), lambda h, j, d: (j * (1 - h) + (tiles - 1) * h, 0)),
                pl.BlockSpec((tile, columns), lambda h, j, d: (j * h, 0)),
            ],
        ),
        out_shape=[half, half],
        compiler_params=params(),
        cost_estimate=cost(2 * block * rows * columns, 6e6),
    )(d, a, b, *others)


def split_low(value):
    high = value.astype(LOW)
    return high, (value - high.astype(F32)).astype(LOW)


def norm_parts(rows):
    rr = lax.rsqrt(jnp.mean(rows * rows, axis=-1, keepdims=True) + EPS)
    return rows * rr, rr


def norm_back(grad, normal, rr, gain):
    weighted = grad * gain
    return rr * (weighted - normal * jnp.mean(weighted * normal, axis=-1, keepdims=True))


def add_all(refs):
    return functools.reduce(jnp.add, [ref[...].astype(F32) for ref in refs])


def pad_rows(rows, count):
    if rows.shape[0] == count:
        return rows
    return jnp.concatenate(
        [rows, jnp.zeros((count - rows.shape[0], rows.shape[1]), rows.dtype)], axis=0
    )


def router_kernel(experts, *refs):
    x_ref, attn_ref, gain_ref, router_ref, mask_ref = refs[:5]
    hidden_ref, mixed_ref, probs_ref = refs[-3:]
    width = x_ref.shape[1]
    lanes = mask_ref.shape[1]
    hidden = add_all([x_ref, attn_ref])
    hidden_ref[...] = hidden
    mixed = (norm_parts(hidden)[0] * gain_ref[...]).astype(LOW)
    mixed_ref[:, :width] = mixed
    logits = dot_nt(mixed, pad_rows(router_ref[...], lanes))
    lane = lax.broadcasted_iota(jnp.int32, logits.shape, 1)
    logits = jnp.where(lane < experts, logits, -1e30)
    weights = jnp.exp(logits - jnp.max(logits, axis=1, keepdims=True))
    probs = weights / jnp.sum(weights, axis=1, keepdims=True)
    probs_ref[...] = probs
    chosen = probs * mask_ref[...]
    high, low = split_low(chosen / jnp.sum(chosen, axis=1, keepdims=True))
    both = high.astype(F32) + pltpu.roll(low.astype(F32), experts, 1)
    mixed_ref[:, width:] = both.astype(LOW)


def route_rows(x, attn, gain, router, mask, experts, others):
    tokens, width = x.shape
    lanes = mask.shape[1]
    operands = [x, attn, gain[None], router, mask]
    shapes = [
        jax.ShapeDtypeStruct((tokens, width), F32),
        jax.ShapeDtypeStruct((tokens, width + lanes), LOW),
        jax.ShapeDtypeStruct((tokens, lanes), F32),
    ]
    return pl.pallas_call(
        functools.partial(router_kernel, experts),
        grid=(1,),
        in_specs=[full(value.shape) for value in operands]
        + [pl.BlockSpec(memory_space=pl.ANY)] * len(others),
        out_specs=[full(shape.shape) for shape in shapes],
        out_shape=shapes,
        compiler_params=params(),
        cost_estimate=cost(2 * tokens * width * lanes, 5e6),
    )(*operands, *others)


def one_hot(slots, count, first):
    groups, tokens = slots.shape
    slot = lax.broadcasted_iota(jnp.int32, (groups, count, tokens), 1).astype(F32)
    same = slots[:, None, :] == slot + float(first)
    return jnp.where(same, 1.0, 0.0).reshape(groups * count, tokens)


def slot_kernel(capacity, meta_ref, col_ref, rows_ref, slots_ref):
    groups, block = slots_ref.shape
    rows, width = rows_ref.shape
    n = rows // groups // capacity
    tokens = block // n
    mask = col_ref[:, width:]
    lanes = mask.shape[1]
    padded = -(-groups // 16) * 16
    group = lax.broadcasted_iota(jnp.int32, (padded, lanes), 0)
    lane = lax.broadcasted_iota(jnp.int32, (padded, lanes), 1)
    wanted = jnp.logical_and(lane == group * n + meta_ref[0], group < groups)
    hits = dot_nt(jnp.where(wanted, 1.0, 0.0).astype(LOW), mask)
    before = lax.broadcasted_iota(jnp.int32, (tokens, tokens), 0)
    after_it = lax.broadcasted_iota(jnp.int32, (tokens, tokens), 1)
    earlier = jnp.where(before < after_it, 1.0, 0.0).astype(LOW)
    for z in range(n):
        hit = hits[:, z * tokens : (z + 1) * tokens]
        rank = dot_nn(hit.astype(LOW), earlier)
        turn = (meta_ref[1 + z] * capacity).astype(F32)
        slot = jnp.where(hit > 0.5, rank + turn, -1.0)
        slots_ref[:, z * tokens : (z + 1) * tokens] = slot[:groups]
    spread = one_hot(slots_ref[...], n * capacity, 0).astype(LOW)
    rows_ref[...] = dot_nn(spread, col_ref[:, :width]).astype(LOW)


def make_slots(meta, col, width, groups, capacity):
    block = col.shape[0]
    n = lax.axis_size("expert")
    shapes = [
        jax.ShapeDtypeStruct((groups * n * capacity, width), LOW),
        jax.ShapeDtypeStruct((groups, block), F32),
    ]
    return pl.pallas_call(
        functools.partial(slot_kernel, capacity),
        grid_spec=pltpu.PrefetchScalarGridSpec(
            num_scalar_prefetch=1,
            grid=(1,),
            in_specs=[full(col.shape)],
            out_specs=[full(shape.shape) for shape in shapes],
        ),
        out_shape=shapes,
        compiler_params=params(),
        cost_estimate=cost(2 * groups * n * capacity * block * width, 8e6),
    )(meta, col)


def table_kernel(capacity, n_half, meta_ref, slots_ref, near_ref, far_ref, near_back_ref, far_back_ref):
    n = 2 * n_half
    tokens = slots_ref.shape[1] // n
    cap_half = n_half * capacity
    for part, (to_ref, back_ref) in enumerate([(near_ref, near_back_ref), (far_ref, far_back_ref)]):
        pieces = []
        for k in range(n_half):
            start = pl.multiple_of(meta_ref[1 + n + part * n_half + k] * tokens, tokens)
            pieces.append(slots_ref[:, pl.ds(start, tokens)])
        spread = one_hot(jnp.concatenate(pieces, axis=1), cap_half, part * cap_half)
        to_ref[...] = spread.astype(LOW)
        back_ref[...] = jnp.transpose(spread).astype(LOW)


def make_tables(meta, slots, n_half, capacity):
    groups, block = slots.shape
    rows = groups * n_half * capacity
    shapes = [jax.ShapeDtypeStruct((rows, block // 2), LOW)] * 2
    shapes += [jax.ShapeDtypeStruct((block // 2, rows), LOW)] * 2
    outs = pl.pallas_call(
        functools.partial(table_kernel, capacity, n_half),
        grid_spec=pltpu.PrefetchScalarGridSpec(
            num_scalar_prefetch=1,
            grid=(1,),
            in_specs=[full(slots.shape)],
            out_specs=[full(shape.shape) for shape in shapes],
        ),
        out_shape=shapes,
        compiler_params=params(),
        cost_estimate=cost(8 * rows * block, 3e6),
    )(meta, slots)
    return outs[:2], outs[2:]


def spread_kernel(choices, place_ref, spread_ref, *refs):
    out_ref, rows_ref = refs[-2:]
    for k, by_place in enumerate(choices):
        for which in sorted(set(by_place)):
            hit = functools.reduce(
                jnp.logical_or,
                [place_ref[0] == i for i, other in enumerate(by_place) if other == which],
            )

            @pl.when(hit)
            def _():
                tokens = refs[which].shape[0]
                rows_ref[k * tokens : (k + 1) * tokens] = refs[which][...]

    out_ref[...] = dot_nn(spread_ref[...], rows_ref[...]).astype(LOW)


def spread_rows(place, spread, found, turns, others):
    n = lax.axis_size("expert")
    order = arrival_order(n)
    distances = sorted({order[i][turn] - i for i in range(n) for turn in turns})
    choices = [[distances.index(order[i][turn] - i) for i in range(n)] for turn in turns]
    chunks = [found[distance] for distance in distances]
    tokens, wide = chunks[0].shape
    rows = spread.shape[0]
    return pl.pallas_call(
        functools.partial(spread_kernel, choices),
        grid_spec=pltpu.PrefetchScalarGridSpec(
            num_scalar_prefetch=1,
            grid=(1,),
            in_specs=[full(spread.shape)]
            + [full(chunk.shape) for chunk in chunks]
            + [pl.BlockSpec(memory_space=pl.ANY)] * len(others),
            out_specs=full((rows, wide)),
            scratch_shapes=[pltpu.VMEM((len(turns) * tokens, wide), LOW)],
        ),
        out_shape=jax.ShapeDtypeStruct((rows, wide), LOW),
        compiler_params=params(),
        cost_estimate=cost(2 * rows * len(turns) * tokens * wide, 5e6),
    )(place, spread, *chunks, *others)


def router_back_kernel(experts, *refs):
    sum_ref, g_ref, hidden_ref, gain_ref, router_ref, mask_ref, probs_ref = refs[:7]
    grad_ref, low_ref, dgain_ref, drouter_ref = refs[-4:]
    width = g_ref.shape[1]
    lanes = mask_ref.shape[1]
    total = sum_ref[...].astype(F32)
    table = total[:, width:]
    mask, probs = mask_ref[...], probs_ref[...]
    grad_gates = (table + pltpu.roll(table, lanes - experts, 1)) * mask
    chosen = probs * mask
    chosen_sum = jnp.sum(chosen, axis=1, keepdims=True)
    mean = jnp.sum(grad_gates * (chosen / chosen_sum), axis=1, keepdims=True)
    centred = mask * (grad_gates - mean) / chosen_sum
    grad_logits = probs * (centred - jnp.sum(centred * chosen, axis=1, keepdims=True))
    high, low = split_low(grad_logits)
    router = pad_rows(router_ref[...], lanes)
    grad = total[:, :width] + dot_nn(high, router) + dot_nn(low, router)
    normal, rr = norm_parts(hidden_ref[...])
    mixed = (normal * gain_ref[...]).astype(LOW)
    drouter_ref[...] = dot_tn(high, mixed) + dot_tn(low, mixed)
    dgain_ref[...] = jnp.sum(grad * normal, axis=0, keepdims=True)
    grad_hidden = g_ref[...].astype(F32) + norm_back(grad, normal, rr, gain_ref[...])
    grad_ref[...] = grad_hidden
    low_ref[...] = grad_hidden.astype(LOW)


def route_back(summed, g, hidden, gain, router, mask, probs, experts, others):
    tokens, width = g.shape
    lanes = mask.shape[1]
    operands = [summed, g, hidden, gain[None], router, mask, probs]
    shapes = [
        jax.ShapeDtypeStruct((tokens, width), F32),
        jax.ShapeDtypeStruct((tokens, width), LOW),
        jax.ShapeDtypeStruct((1, width), F32),
        jax.ShapeDtypeStruct((lanes, width), F32),
    ]
    return pl.pallas_call(
        functools.partial(router_back_kernel, experts),
        grid=(1,),
        in_specs=[full(value.shape) for value in operands]
        + [pl.BlockSpec(memory_space=pl.ANY)] * len(others),
        out_specs=[full(shape.shape) for shape in shapes],
        out_shape=shapes,
        compiler_params=params(),
        cost_estimate=cost(8 * tokens * width * lanes, 8e6),
    )(*operands, *others)


def combine_kernel(meta_ref, table_ref, rows_ref, *rest):
    del meta_ref
    rest[-1][...] = dot_nn(table_ref[...], rows_ref[...]).astype(LOW)


def combine_part(meta, table, rows, first, n, into, others):
    block, slots = table.shape
    wide = rows.shape[1]
    tokens = block // (n // 2)
    return pl.pallas_call(
        combine_kernel,
        grid_spec=pltpu.PrefetchScalarGridSpec(
            num_scalar_prefetch=1,
            grid=(n // 2,),
            in_specs=[
                pl.BlockSpec((tokens, slots), lambda i, m: (i, 0)),
                full(rows.shape),
            ]
            + [pl.BlockSpec(memory_space=pl.ANY)] * (len(into) + len(others)),
            out_specs=pl.BlockSpec((tokens, wide), lambda i, m: (m[1 + n + first + i], 0)),
        ),
        out_shape=jax.ShapeDtypeStruct((n * tokens, wide), LOW),
        input_output_aliases={3: 0} if into else {},
        compiler_params=params(),
        cost_estimate=cost(2 * slots * block * wide, 6e6),
    )(meta, table, rows, *into, *others)


def combine_rows(meta, tables, rows, n_half, others):
    near = combine_part(meta, tables[0], rows[0], 0, 2 * n_half, [], [])
    return combine_part(meta, tables[1], rows[1], n_half, 2 * n_half, [near], others)


def expert_kernel(experts, who_ref, x_ref, gate_ref, up_ref, pull_ref, *rest):
    act_ref, dgate_ref, dup_ref, copy_ref = rest[-4:]
    width = gate_ref.shape[0]
    x = x_ref[:, :width]
    table = x_ref[:, width:].astype(F32)
    lane = lax.broadcasted_iota(jnp.int32, table.shape, 1)
    mine = who_ref[0]
    gate = jnp.sum(
        jnp.where(jnp.logical_or(lane == mine, lane == mine + experts), table, 0.0),
        axis=1,
        keepdims=True,
    )
    pre_gate = dot_nn(x, gate_ref[...])
    pre_up = dot_nn(x, up_ref[...])
    pull = pull_ref[...].reshape(pre_up.shape)
    sig = 1.0 / (1.0 + jnp.exp(-pre_gate))
    silu = pre_gate * sig
    act = silu * pre_up
    act_ref[...] = (act * gate).astype(LOW)
    high, low = split_low(jnp.sum(act * pull, axis=1, keepdims=True))
    pull = pull * gate
    dup = (pull * silu).astype(LOW)
    dgate = (pull * pre_up * (sig * (1.0 + pre_gate * (1.0 - sig)))).astype(LOW)
    dgate_ref[...] = dgate
    dup_ref[...] = dup
    copy_ref[:, :width] = (dot_nt(dgate, gate_ref[...]) + dot_nt(dup, up_ref[...])).astype(LOW)
    back = jnp.where(lane == mine, high.astype(F32), 0.0)
    back = jnp.where(lane == mine + experts, low.astype(F32), back)
    copy_ref[:, width:] = back.astype(LOW)


def run_expert(who, x, w_gate, w_up, pull, part, experts):
    rows, wide = x.shape
    width, hidden = w_gate.shape
    groups, _, slots, _ = pull.shape
    each = groups // 2
    tile = each * slots
    by_rows = lambda columns: pl.BlockSpec((tile, columns), lambda i, p: (i, 0))
    return pl.pallas_call(
        functools.partial(expert_kernel, experts),
        grid_spec=pltpu.PrefetchScalarGridSpec(
            num_scalar_prefetch=1,
            grid=(2,),
            in_specs=[
                by_rows(wide),
                full(w_gate.shape),
                full(w_up.shape),
                pl.BlockSpec((each, 1, slots, hidden), lambda i, p: (i, part, 0, 0)),
            ],
            out_specs=[by_rows(hidden), by_rows(hidden), by_rows(hidden), by_rows(wide)],
        ),
        out_shape=[jax.ShapeDtypeStruct((rows, hidden), LOW)] * 3
        + [jax.ShapeDtypeStruct((rows, wide), LOW)],
        compiler_params=params(),
        cost_estimate=cost(8 * rows * width * hidden, 20e6, rows * hidden),
    )(who, x, w_gate, w_up, pull)


def input_kernel(grad_ref, x_ref, gain_ref, more_ref, out_ref):
    normal, rr = norm_parts(x_ref[...].astype(F32))
    grad = grad_ref[...].astype(F32)
    out_ref[...] = more_ref[...] + norm_back(grad, normal, rr, gain_ref[...])


def input_back(grad, x, gain, more):
    tokens, width = x.shape
    operands = [grad, x, gain[None], more]
    return pl.pallas_call(
        input_kernel,
        grid=(1,),
        in_specs=[full(value.shape) for value in operands],
        out_specs=full(more.shape),
        out_shape=jax.ShapeDtypeStruct((tokens, width), F32),
        compiler_params=params(),
        cost_estimate=cost(20 * tokens * width, 5e6),
    )(*operands)


def kv_back_kernel(factor, parts_ref, proj_ref, gain_ref, cos_ref, sin_ref, *rest):
    grad_ref, dgain_ref = rest[-2:]
    size = proj_ref.shape[1]
    total = parts_ref[0].astype(F32)
    for k in range(1, parts_ref.shape[0]):
        total += parts_ref[k].astype(F32)
    grad, dgain = head_backward(
        total[:, :size] * factor, proj_ref[...], gain_ref[...], cos_ref[...], sin_ref[...]
    )
    grad_ref[:, :size] = grad.astype(LOW)
    grad_ref[:, size:] = total[:, size:].astype(LOW)
    dgain_ref[...] = dgain


def kv_back(parts, proj, gain, cos2, sin2, factor, others):
    block, size = proj.shape
    operands = [parts, proj, gain[None], cos2, sin2]
    shapes = [
        jax.ShapeDtypeStruct((block, 2 * size), LOW),
        jax.ShapeDtypeStruct((1, size), F32),
    ]
    return pl.pallas_call(
        functools.partial(kv_back_kernel, factor),
        grid=(1,),
        in_specs=[full(value.shape) for value in operands]
        + [pl.BlockSpec(memory_space=pl.ANY)] * len(others),
        out_specs=[full(shape.shape) for shape in shapes],
        out_shape=shapes,
        compiler_params=params(),
        cost_estimate=cost(40 * block * size, 5e6),
    )(*operands, *others)


def pair_kernel(a_ref, b_ref, *rest):
    rest[-1][...] = (a_ref[...].astype(F32) + b_ref[...].astype(F32)).astype(LOW)


def pair_sum(a, b, others):
    rows, columns = a.shape
    tiles = 2 if rows % 32 == 0 else 1
    spec = pl.BlockSpec((rows // tiles, columns), lambda i: (i, 0))
    return pl.pallas_call(
        pair_kernel,
        grid=(tiles,),
        in_specs=[spec, spec] + [pl.BlockSpec(memory_space=pl.ANY)] * len(others),
        out_specs=spec,
        out_shape=jax.ShapeDtypeStruct((rows, columns), LOW),
        compiler_params=params(),
        cost_estimate=cost(rows * columns, 6 * rows * columns),
    )(a, b, *others)


def fold_kernel(n_pairs, s_ref, *refs):
    del s_ref
    send_ref, keep_ref = refs[-2:]
    totals = [
        (refs[2 * k][...].astype(F32) + refs[2 * k + 1][...].astype(F32)).astype(LOW)
        for k in range(n_pairs)
    ]
    for half, out_ref in enumerate((send_ref, keep_ref)):

        @pl.when(pl.program_id(0) == half)
        def _():
            first = 0
            for total in totals:
                last = first + total.shape[1]
                out_ref[:, first:last] = total
                first = last


def fold(pairs, bit, others):
    rows = pairs[0][1].shape[0]
    columns = sum(got.shape[1] for _, got in pairs)
    tiles = 2
    tile = rows // (2 * tiles)
    side = lambda h, m: (1 - m[0]) * (1 - h) + m[0] * h
    specs = []
    for _, got in pairs:
        wide = got.shape[1]
        specs += [pl.BlockSpec((tile, wide), lambda h, j, m: (side(h, m) * tiles + j, 0))] * 2
    shape = jax.ShapeDtypeStruct((rows // 2, columns), LOW)
    return pl.pallas_call(
        functools.partial(fold_kernel, len(pairs)),
        grid_spec=pltpu.PrefetchScalarGridSpec(
            num_scalar_prefetch=1,
            grid=(2, tiles),
            in_specs=specs + [pl.BlockSpec(memory_space=pl.ANY)] * len(others),
            out_specs=[
                pl.BlockSpec((tile, columns), lambda h, j, m: (j * (1 - h) + (tiles - 1) * h, 0)),
                pl.BlockSpec((tile, columns), lambda h, j, m: (j * h, 0)),
            ],
        ),
        out_shape=[shape, shape],
        compiler_params=params(),
        cost_estimate=cost(rows * columns, 6 * rows * columns),
    )(
        bit.astype(jnp.int32)[None],
        *[value for pair in pairs for value in pair],
        *others,
    )


def normed_kernel(q_ref, kv_ref, wq_ref, wkv_ref, rows_ref, *rest):
    out_ref, dgain_ref = rest[-2:]
    grad = dot_nt(q_ref[...], wq_ref[...]) + dot_nt(kv_ref[...], wkv_ref[...])
    out_ref[...] = grad.astype(LOW)
    dgain_ref[...] = jnp.sum(grad * rows_ref[...].astype(F32), axis=0, keepdims=True)


def normed_back(grad_q, grad_kv, w_q, w_kv, rows, others):
    block, width = rows.shape
    tile = 512
    column = lambda i: (0, i)
    return pl.pallas_call(
        normed_kernel,
        grid=(width // tile,),
        in_specs=[
            full(grad_q.shape),
            full(grad_kv.shape),
            pl.BlockSpec((tile, w_q.shape[1]), lambda i: (i, 0)),
            pl.BlockSpec((tile, w_kv.shape[1]), lambda i: (i, 0)),
            pl.BlockSpec((block, tile), column),
        ]
        + [pl.BlockSpec(memory_space=pl.ANY)] * len(others),
        out_specs=[pl.BlockSpec((block, tile), column), pl.BlockSpec((1, tile), column)],
        out_shape=[
            jax.ShapeDtypeStruct((block, width), LOW),
            jax.ShapeDtypeStruct((1, width), F32),
        ],
        compiler_params=params(),
        cost_estimate=cost(2 * block * width * (w_q.shape[1] + w_kv.shape[1]), 12e6),
    )(grad_q, grad_kv, w_q, w_kv, rows, *others)


def pack_kernel(experts, router_ref, attn_ref, gain_ref, mlp_ref, q_ref, k_ref, *rest):
    out_ref, rows_ref = rest[-2:]
    size = q_ref.shape[1]
    rows_ref[:experts] = router_ref[:experts]
    rows_ref[experts:] = jnp.zeros_like(rows_ref[experts:])
    rows_ref[experts : experts + 1] = attn_ref[...] / gain_ref[...]
    rows_ref[experts + 1 : experts + 2] = mlp_ref[...]
    rows_ref[experts + 2 : experts + 3, :size] = q_ref[...]
    rows_ref[experts + 2 : experts + 3, size : 2 * size] = k_ref[...]
    out_ref[...] = rows_ref[...].astype(LOW)


def pack_small(experts, router, attn, gain, mlp, q, k, others):
    width = attn.shape[1]
    n = lax.axis_size(ALL_AXES)
    shape = (-(-(experts + 3) // n) * n, width)
    operands = [router, attn, gain[None], mlp, q, k]
    return pl.pallas_call(
        functools.partial(pack_kernel, experts),
        grid=(1,),
        in_specs=[full(value.shape) for value in operands]
        + [pl.BlockSpec(memory_space=pl.ANY)] * len(others),
        out_specs=full(shape),
        out_shape=jax.ShapeDtypeStruct(shape, LOW),
        scratch_shapes=[pltpu.VMEM(shape, F32)],
        compiler_params=params(),
        cost_estimate=cost(shape[0] * width, 6 * shape[0] * width),
    )(*operands, *others)


def part_sum_kernel(parts_ref, *rest):
    total = parts_ref[0].astype(F32)
    for k in range(1, parts_ref.shape[0]):
        total += parts_ref[k].astype(F32)
    rest[-1][...] = total.astype(LOW)


def part_sum(parts, others):
    count, rows, columns = parts.shape
    tiles = 2
    return pl.pallas_call(
        part_sum_kernel,
        grid=(tiles,),
        in_specs=[pl.BlockSpec((count, rows // tiles, columns), lambda i: (0, i, 0))]
        + [pl.BlockSpec(memory_space=pl.ANY)] * len(others),
        out_specs=pl.BlockSpec((rows // tiles, columns), lambda i: (i, 0)),
        out_shape=jax.ShapeDtypeStruct((rows, columns), LOW),
        compiler_params=params(),
        cost_estimate=cost(count * rows * columns, 4 * count * rows * columns),
    )(parts, *others)


def widen_kernel(n_chunks, n_outs, at_ref, *refs):
    del at_ref
    outs = refs[-n_outs:]
    widths = [ref.shape[1] for ref in outs]
    for k in range(n_chunks):

        @pl.when(pl.program_id(0) == k)
        def _():
            first = 0
            for wide, out_ref in zip(widths, outs):
                out_ref[...] = refs[k][:, first : first + wide].astype(F32)
                first += wide


def widen(places, chunks, widths, total, into, others):
    rows, columns = chunks[0].shape
    count = len(chunks)
    return pl.pallas_call(
        functools.partial(widen_kernel, count, len(widths)),
        grid_spec=pltpu.PrefetchScalarGridSpec(
            num_scalar_prefetch=1,
            grid=(count,),
            in_specs=[full(chunk.shape) for chunk in chunks]
            + [pl.BlockSpec(memory_space=pl.ANY)] * (len(into) + len(others)),
            out_specs=[pl.BlockSpec((rows, wide), lambda i, at: (at[i], 0)) for wide in widths],
        ),
        out_shape=[jax.ShapeDtypeStruct((total, wide), F32) for wide in widths],
        input_output_aliases={1 + count + k: k for k in range(len(into))},
        compiler_params=params(),
        cost_estimate=cost(rows * columns, 6 * count * rows * columns),
    )(jnp.stack(places).astype(jnp.int32), *chunks, *into, *others)


def swap_dp(rows):
    return lax.ppermute(rows, "dp", [(0, 1), (1, 0)])


def swap_context(rows, s):
    n = lax.axis_size("context")
    return lax.ppermute(rows, "context", [(i, i ^ s) for i in range(n)])


def share_context(parts):
    return lax.all_to_all(parts, "context", split_axis=0, concat_axis=0, tiled=True)


def plane_turns():
    d, c = lax.axis_index("dp"), lax.axis_index("context")
    low, high = lax.rem(c, 2), lax.div(c, 2)

    def swap(first, second):
        perm = [(i, i ^ first) for i in range(4)] + [(4 + i, 4 + (i ^ second)) for i in range(4)]
        return lambda rows: lax.ppermute(rows, GROUP_AXES, perm)

    return [
        (jnp.where(d == 0, low, high), swap(1, 2)),
        (jnp.where(d == 0, high, low), swap(2, 1)),
    ]


def plane_first(pairs, others):
    (bit_1, _), _ = plane_turns()
    return fold(pairs, bit_1, others)


def plane_second(send, keep, others):
    (_, swap_1), (bit_2, _) = plane_turns()
    return fold([(keep, swap_1(send))], bit_2, others)


def plane_last(send, keep, others):
    _, (_, swap_2) = plane_turns()
    return pair_sum(keep, swap_2(send), others)


def plane_spread(own):
    (_, swap_1), (_, swap_2) = plane_turns()
    second = swap_2(own)
    return [own, second, swap_1(own), swap_1(second)]


def quarter_places(rank):
    d = lax.axis_index("dp")
    c = lax.axis_index("context")
    low, high = lax.rem(c, 2), lax.div(c, 2)
    places = []
    for core in (d, 1 - d):
        bit_1 = jnp.where(core == 0, low, high)
        bit_2 = jnp.where(core == 0, high, low)
        for flip_1, flip_2 in ((0, 0), (0, 1), (1, 0), (1, 1)):
            places.append(4 * core + rank(core, bit_1 ^ flip_1, bit_2 ^ flip_2))
    return places


def widen_all(quarters, places, widths, others):
    count = len(quarters)
    total = 2 * count * quarters[0].shape[0]
    swapped = [swap_dp(part) for part in quarters]
    here = widen(places[:count], quarters, widths, total, [], [])
    return widen(places[count:], swapped, widths, total, here, others)


def arrival_order(n):
    return [sorted(range(n), key=lambda j: (abs(j - i), j)) for i in range(n)]


def choose(index, options):
    distinct = []
    for option in options:
        if option is not None and not any(option is other for other in distinct):
            distinct.append(option)
    result = distinct[0]
    for option in distinct[1:]:
        mask = functools.reduce(
            jnp.logical_or, [index == i for i, other in enumerate(options) if other is option]
        )
        result = jnp.where(mask, option, result)
    return result


def line_gather(chunk):
    return line_steps({0: chunk}, 1, lax.axis_size("expert"))


def line_steps(found, first, stop):
    n = lax.axis_size("expert")
    found = dict(found)
    for s in range(first, stop):
        found[-s] = lax.ppermute(
            found[1 - s], "expert", [(i, i + 1) for i in range(s - 1, n - 1)]
        )
        found[s] = lax.ppermute(found[s - 1], "expert", [(i + 1, i) for i in range(n - s)])
    return found


def context_gather(rows):
    n = lax.axis_size("context")
    c = lax.axis_index("context")
    found = {0: rows}
    for s in range(1, n):
        found[s] = lax.ppermute(rows, "context", [(i, i ^ s) for i in range(n)])
    return jnp.concatenate([choose(c, [found[i ^ j] for i in range(n)]) for j in range(n)], axis=0)


def zero_of(*others):
    return functools.reduce(
        jnp.add,
        [
            lax.slice(other, (0,) * other.ndim, (1,) * other.ndim).reshape(()).astype(F32) * 0.0
            for other in others
        ],
    )


def after(value, *others):
    return (value.astype(F32) + zero_of(*others)).astype(value.dtype)


def on_device(
    layer_input,
    grad_output,
    attn_gain,
    query_weight,
    key_weight,
    value_weight,
    q_gain,
    k_gain,
    output_weight,
    mlp_gain,
    router,
    w_gate,
    w_up,
    w_down,
    routes,
    half_order,
):
    n_context = lax.axis_size("context")
    n_expert = lax.axis_size("expert")
    n_groups = lax.axis_size(GROUP_AXES)
    tok_dev, width = layer_input.shape[1:]
    size = q_gain.shape[0]
    kv_total = key_weight.shape[1] * n_expert
    group_dev = n_expert // (kv_total // size)
    kv_index = lax.axis_index("expert") // group_dev
    block = tok_dev * n_expert
    seq = block * n_context
    half = block // 2
    experts = router.shape[1]
    exp_dev = w_gate.shape[0]
    top = routes.shape[2]
    capacity = max(2, (tok_dev * top * 9 + 8 * experts - 1) // (8 * experts))
    scale = size ** (-0.5)

    seq_rows = jnp.arange(seq, dtype=jnp.int32)
    context = lax.axis_index("context")
    own_halves = lax.dynamic_slice_in_dim(half_order, 2 * context, 2)
    own_pos = (own_halves[:, None] * half + jnp.arange(half, dtype=jnp.int32)[None]).reshape(-1)
    per_half = half // TILE
    tile_pos = (half_order[:, None] * per_half + jnp.arange(per_half, dtype=jnp.int32)).reshape(-1)
    kidx = jnp.sum(
        (tile_pos[None, :] == jnp.arange(seq // TILE, dtype=jnp.int32)[:, None])
        * jnp.arange(seq // TILE, dtype=jnp.int32)[None, :],
        axis=1,
    ).astype(jnp.int32)
    qpos = lax.dynamic_slice_in_dim(tile_pos, context * (block // TILE), block // TILE)
    entry = jnp.arange(size)
    freq = jnp.power(THETA, -(2 * (entry % (size // 2))).astype(F32) / size)
    angles = own_pos.astype(F32)[:, None] * freq[None, :]
    cos2 = jnp.cos(angles)
    sin2 = jnp.sin(angles) * jnp.where(entry < size // 2, -1.0, 1.0)[None, :]

    place = lax.axis_index("expert")
    place_1 = place.astype(jnp.int32)[None]
    lanes = -(-2 * experts // 128) * 128
    mask = jnp.any(
        routes[0][:, :, None] == jnp.arange(lanes, dtype=jnp.int32)[None, None, :], axis=1
    )
    mask_wide = mask.astype(F32)
    router_rows = router.T

    x_low = layer_input[0]
    x_normal, _ = norm_parts(x_low.astype(F32))
    normed_found = line_gather((x_normal * attn_gain).astype(LOW))
    if group_dev == 1:
        kv_weights = jnp.concatenate([key_weight, value_weight], axis=1)
    else:
        key_whole = lax.all_gather(key_weight, "expert", axis=1, tiled=True)
        value_whole = lax.all_gather(value_weight, "expert", axis=1, tiled=True)
        kv_weights = jnp.concatenate(
            [
                lax.dynamic_slice_in_dim(key_whole, kv_index * size, size, 1),
                lax.dynamic_slice_in_dim(value_whole, kv_index * size, size, 1),
            ],
            axis=1,
        )
    grad_low = grad_output[0]
    normed_rows, own_kv, key_proj, grad_wide = project_keys(
        place_1,
        normed_found,
        kv_weights,
        k_gain,
        cos2,
        sin2,
        scale * LOG2E,
        grad_low,
        mask_wide,
    )
    grad_col = lax.all_gather(grad_wide, "expert", axis=0, tiled=True)
    kv_whole = context_gather(own_kv)
    queries, query_proj = project_queries(normed_rows, query_weight, q_gain, cos2, sin2)

    n_half = n_expert // 2
    order_here = jnp.asarray(arrival_order(n_expert), jnp.int32)[place]
    turn_here = jnp.sum(
        (order_here[:, None] == jnp.arange(n_expert, dtype=jnp.int32)[None, :])
        * jnp.arange(n_expert, dtype=jnp.int32)[:, None],
        axis=0,
    ).astype(jnp.int32)
    meta = jnp.concatenate([place_1, turn_here, order_here])
    grad_sent, slots = make_slots(meta, grad_col, width, n_groups, capacity)
    spreads, back_tables = make_tables(meta, slots, n_half, capacity)

    def swap_plane(rows):
        parts = rows.reshape(n_groups, -1, rows.shape[1])
        parts = lax.all_to_all(parts, GROUP_AXES, split_axis=0, concat_axis=0, tiled=True)
        return parts.reshape(rows.shape)

    attended, inverse = attend(qpos, kidx, queries, kv_whole, [])
    keys_t = kv_whole[:, :size].T
    attn_part = out_dot(attended, output_weight, [grad_col])
    attn_rows = lax.psum_scatter(attn_part, "expert", scatter_dimension=0, tiled=True)

    grad_x = swap_plane(grad_sent)
    act_pull = dot_nt(grad_x, w_down[0]).reshape(n_groups, 2, n_half * capacity, -1)

    hidden, mixed, probs = route_rows(
        x_low, attn_rows, mlp_gain, router_rows, mask_wide, experts, [keys_t]
    )

    who = (lax.axis_index(ALL_AXES) * exp_dev).astype(jnp.int32)[None]
    mixed_found = line_gather(mixed)
    near = spread_rows(place_1, spreads[0], mixed_found, range(n_half), [grad_x])
    x_near = swap_plane(near)
    worked_near = run_expert(who, x_near, w_gate[0], w_up[0], act_pull, 0, experts)
    far = spread_rows(place_1, spreads[1], mixed_found, range(n_half, n_expert), [x_near])
    x_far = swap_plane(far)
    worked_far = run_expert(who, x_far, w_gate[0], w_up[0], act_pull, 1, experts)
    xs = [x_near, x_far]
    acts, gate_lows, up_lows, copies = (list(pair) for pair in zip(worked_near, worked_far))
    back_far = swap_plane(copies[1])
    back_near = swap_plane(copies[0])
    join = lambda parts: jnp.concatenate(parts, axis=0)
    x_all = join([x[:, :width] for x in xs])
    grad_w_gate = dot_tn(x_all, join(gate_lows))
    grad_w_up = dot_tn(x_all, join(up_lows))
    grad_by_round = jnp.swapaxes(
        grad_x.reshape(n_groups, 2, n_half * capacity, width), 0, 1
    ).reshape(-1, width)
    grad_w_down = dot_tn(join(acts), grad_by_round)
    copies_col = combine_rows(
        meta, back_tables, [back_near, back_far], n_half, [grad_w_gate, grad_w_up]
    )
    copies_sum = lax.psum_scatter(copies_col, "expert", scatter_dimension=0, tiled=True)

    returned = [dot_nn(act, w_down[0]).astype(LOW) for act in acts]
    returned_near = swap_plane(returned[0])

    grad_hidden, grad_hidden_low, grad_mlp_gain, grad_router = route_back(
        copies_sum,
        grad_low,
        hidden,
        mlp_gain,
        router_rows,
        mask_wide,
        probs,
        experts,
        [returned_near, grad_w_down],
    )

    returned_far = swap_plane(returned[1])
    grad_attn = lax.all_gather(grad_hidden_low, "expert", axis=0, tiled=True)
    grad_o, centre = grad_attended(
        grad_attn, output_weight, attended, inverse, [returned_far]
    )
    combined = combine_rows(meta, back_tables, [returned_near, returned_far], n_half, [])
    output_rows = lax.psum_scatter(combined, "expert", scatter_dimension=0, tiled=True)
    w_out_send, w_out_keep = token_halves(attended, grad_attn, [combined])
    w_out_half = pair_sum(w_out_keep, swap_dp(w_out_send), [grad_o])
    w_out_parts = share_context(w_out_half.reshape(n_context, -1, width))
    grad_kv, grad_q, grad_q_gain = attend_back(
        qpos,
        kidx,
        queries,
        grad_o,
        centre,
        kv_whole,
        keys_t,
        query_proj,
        q_gain,
        cos2,
        sin2,
        [w_out_half],
    )
    kv_parts = share_context(grad_kv.astype(LOW).reshape(n_context, block, 2 * size))
    w_out_own = part_sum(w_out_parts, [grad_kv])
    w_query_send, w_query_keep = token_halves(normed_rows, grad_q, [w_out_own])
    w_query_got = swap_dp(w_query_send)
    output_rows = hidden + output_rows.astype(F32) + zero_of(w_query_keep)

    kv_grads, grad_k_gain = kv_back(
        kv_parts, key_proj, k_gain, cos2, sin2, scale, [w_query_keep]
    )
    w_out_quarters = plane_spread(w_out_own)
    pairs = [(w_query_keep, w_query_got)]
    widths = [query_weight.shape[1]]
    if group_dev == 1:
        w_kv_send, w_kv_keep = token_halves(normed_rows, kv_grads, w_out_quarters[1:3])
        pairs.append((w_kv_keep, swap_dp(w_kv_send)))
        widths += [key_weight.shape[1], value_weight.shape[1]]
    grad_normed, gain_rows = normed_back(
        grad_q, kv_grads, query_weight, kv_weights, normed_rows, []
    )
    send, keep = plane_first(pairs, [*w_out_quarters, grad_normed])
    (grad_w_out,) = widen_all(
        w_out_quarters,
        quarter_places(lambda core, b1, b2: jnp.where(core == 0, b1 + 2 * b2, 2 * b1 + b2)),
        [width],
        [],
    )
    small = pack_small(
        experts,
        grad_router,
        gain_rows,
        attn_gain,
        grad_mlp_gain,
        grad_q_gain,
        grad_k_gain,
        [],
    )
    swap_all = lambda rows: lax.all_to_all(rows, ALL_AXES, split_axis=0, concat_axis=0, tiled=True)
    small_parts = swap_all(small.reshape(lax.axis_size(ALL_AXES), -1, width))
    small_own = jnp.sum(small_parts.astype(F32), axis=0).astype(LOW)
    second_send, second_keep = plane_second(send, keep, [small])
    quarter = plane_last(second_send, second_keep, [output_rows, small_own])
    grad_normed = lax.psum_scatter(grad_normed, "expert", scatter_dimension=0, tiled=True)
    grad_input = input_back(grad_normed, x_low, attn_gain, grad_hidden)
    small_sum = swap_all(jnp.broadcast_to(small_own[None], small_parts.shape))
    small_sum = small_sum.reshape(small.shape).astype(F32) + zero_of(grad_w_out, grad_input)
    quarters = [quarter] + [swap_context(quarter, s) for s in range(1, n_context)]
    d = lax.axis_index("dp")
    turned = lambda core, c: jnp.where(core == 0, 2 * lax.rem(c, 2) + lax.div(c, 2), c)
    places = [4 * core + turned(core, context ^ s) for core in (d, 1 - d) for s in range(n_context)]
    grad_w_query, *more = widen_all(quarters, places, widths, [small_sum])
    if group_dev == 1:
        grad_w_key, grad_w_value = more
    else:
        w_kv = token_dot(normed_rows, kv_grads, [])
        blank = jnp.zeros((width, kv_total), LOW)
        pieces = []
        for part in (w_kv[:, :size], w_kv[:, size:]):
            padded = lax.dynamic_update_slice(blank, part, (0, kv_index * size))
            pieces.append(lax.psum_scatter(padded, "expert", scatter_dimension=1, tiled=True))
        grad_w_key, grad_w_value = (lax.psum(piece, GROUP_AXES).astype(F32) for piece in pieces)
    grad_attn_gain, grad_mlp_gain = small_sum[experts], small_sum[experts + 1]
    grad_q_gain = small_sum[experts + 2, :size]
    grad_k_gain = small_sum[experts + 2, size : 2 * size]
    return (
        output_rows.astype(LOW)[None],
        grad_input[None],
        grad_attn_gain,
        grad_w_query,
        grad_w_key,
        grad_w_value,
        grad_q_gain,
        grad_k_gain,
        grad_w_out,
        grad_mlp_gain,
        small_sum[:experts].T,
        grad_w_gate[None],
        grad_w_up[None],
        grad_w_down[None],
    )


def solution(mesh):
    rows = P("dp", ("context", "expert"), None)
    expert = P(ALL_AXES, None, None)
    columns = P(None, "expert")
    in_specs = (
        rows,
        rows,
        P(),
        columns,
        columns,
        columns,
        P(),
        P(),
        P("expert", None),
        P(),
        P(),
        expert,
        expert,
        expert,
        rows,
        P(),
    )
    out_specs = (
        rows,
        rows,
        P(),
        columns,
        columns,
        columns,
        P(),
        P(),
        P("expert", None),
        P(),
        P(),
        expert,
        expert,
        expert,
    )
    return jax.shard_map(
        on_device, mesh=mesh, in_specs=in_specs, out_specs=out_specs, check_vma=False
    )
```

profile of v0, /device:TPU:0, one launch (start us, length us, event | category | flops | bytes accessed | tf_op | source)
XLA Modules:
  0.0 642.2 jit_solution(10554282191272858372)
XLA Ops:
  12.0 6.4 collective-permute-start
  19.4 8.5 %collective-permute-done.3.refs_4_ = bf16[128,2048]{1,0:T(8,128)(2,1)} collective-permute-done((bf16[128,2048]{1,0:T(8,128)(2,1)}, bf16[128,2048]{1,0:T(8,128)(2,1)}, u32[]{:S(2)}, u32[]{:S(2)}) %collective-permute-start.3) | collective-permute-done | bytes 524320 | tf_op jit(solution)/shard_map/ppermute | solution.py:1138
  33.8 9.3 %collective-permute-done.4.refs_5_ = bf16[128,2048]{1,0:T(8,128)(2,1)} collective-permute-done((bf16[128,2048]{1,0:T(8,128)(2,1)}, bf16[128,2048]{1,0:T(8,128)(2,1)}, u32[]{:S(2)}, u32[]{:S(2)}) %collective-permute-start.4) | collective-permute-done | bytes 524320 | tf_op jit(solution)/shard_map/ppermute | solution.py:1138
  50.2 7.3 %collective-permute-done.5.refs_6_ = bf16[128,2048]{1,0:T(8,128)(2,1)} collective-permute-done((bf16[128,2048]{1,0:T(8,128)(2,1)}, bf16[128,2048]{1,0:T(8,128)(2,1)}, u32[]{:S(2)}, u32[]{:S(2)}) %collective-permute-start.5) | collective-permute-done | bytes 524320 | tf_op jit(solution)/shard_map/ppermute | solution.py:1138
  57.5 4.9 shard_map.272
  67.9 9.0 %shard_map.273 = (bf16[2,8,256,128]{3,2,1,0:T(8,128)(2,1)}, f32[2,8,256,128]{3,2,1,0:T(8,128)}) custom-call(bf16[512,2048]{1,0:T(8,128)(2,1)} %get-tuple-element.68.x_ref.a_ref.rows_ref, bf16[2048,1024]{1,0:T(8,128)(2,1)} %wq_ref.1, f32[1,128]{1,0:T(1,128)} %bitcast.134, f32[512,128]{1,0:T(8,128)} %get-tuple-element.135.refs_9_.cos_ref, ...), custom_call_target="tpu_custom_call" | custom-call | flops 2147483648 | bytes 12000000 | tf_op jit(solution)/shard_map/pallas_call | solution.py:76
  80.3 11.6 %shard_map.274 = (bf16[512,1024]{1,0:T(8,128)(2,1)}, f32[2,8,256,128]{3,2,1,0:T(8,128)}) custom-call(s32[2]{0:T(128)} %get-tuple-element.125.qpos_ref, s32[8]{0:T(128)} %select_reduce_fusion.kidx_ref, bf16[2,8,256,128]{3,2,1,0:T(8,128)(2,1)} %get-tuple-element.69.q_ref, bf16[2048,256]{1,0:T(8,128)(2,1)} %copy.66.kv_ref), custom_call_target="tpu_custom_call" | custom-call | flops 6442450944 | bytes 8000000 | tf_op jit(solution)/shard_map/pallas_call | solution.py:198
  91.9 22.0 %all-gather.3.cloned.1.call-done.rest_0_.col_ref = bf16[512,2176]{1,0:T(8,128)(2,1)} async-done(((bf16[128,2176]{1,0:T(8,128)(2,1)}), bf16[512,2176]{1,0:T(8,128)(2,1)}) %all-gather.3.cloned.1.call-update) | async-done | bytes 2228240 | tf_op jit(solution)/shard_map/all_gather | solution.py:1254
  114.0 6.0 shard_map.275
  121.3 7.3 %shard_map.277 = (bf16[1152,2048]{1,0:T(8,128)(2,1)}, f32[8,512]{1,0:T(8,128)}) custom-call(s32[9]{0:T(128)} %pad_add_fusion.meta_ref, bf16[512,2176]{1,0:T(8,128)(2,1)} %all-gather.3.cloned.1.call-done.rest_0_.col_ref), custom_call_target="tpu_custom_call" | custom-call | flops 2415919104 | bytes 8000000 | tf_op jit(solution)/shard_map/pallas_call | solution.py:572
  128.7 4.8 all-to-all-start
  135.4 27.5 %reduce-scatter.5.cloned.1.call-done.refs_1_ = bf16[128,2048]{1,0:T(8,128)(2,1)} async-done(((bf16[512,2048]{1,0:T(8,128)(2,1)}), bf16[128,2048]{1,0:T(8,128)(2,1)}) %reduce-scatter.5.cloned.1.call-update) | async-done | bytes 524304 | tf_op jit(solution)/shard_map/reduce_scatter | solution.py:1277
  167.1 5.4 collective-permute-start.9
  175.0 12.7 %all-to-all-done = bf16[8,144,2048]{2,1,0:T(8,128)(2,1)} async-done(((bf16[8,144,2048]{2,1,0:T(8,128)(2,1)}), bf16[8,144,2048]{2,1,0:T(8,128)(2,1)}, u32[]{:S(2)}, u32[]{:S(2)}) %all-to-all-start) | async-done | bytes 4718624 | tf_op jit(solution)/shard_map/all_to_all | solution.py:1271
  198.0 15.0 %collective-permute-done.13.refs_3_ = bf16[128,2176]{1,0:T(8,128)(2,1)S(1)} collective-permute-done((bf16[128,2176]{1,0:T(8,128)(2,1)}, bf16[128,2176]{1,0:T(8,128)(2,1)S(1)}, u32[]{:S(2)}, u32[]{:S(2)}) %collective-permute-start.13) | collective-permute-done | bytes 557088 | tf_op jit(solution)/shard_map/ppermute | solution.py:1138
  216.6 13.2 %collective-permute-done.14.refs_4_ = bf16[128,2176]{1,0:T(8,128)(2,1)S(1)} collective-permute-done((bf16[128,2176]{1,0:T(8,128)(2,1)S(1)}, bf16[128,2176]{1,0:T(8,128)(2,1)S(1)}, u32[]{:S(2)}, u32[]{:S(2)}) %collective-permute-start.14) | collective-permute-done | bytes 557088 | tf_op jit(solution)/shard_map/ppermute | solution.py:1138
  239.2 8.0 %fusion.pull_ref = f32[8,2,72,768]{3,2,1,0:T(8,128)} fusion(bf16[8,2,72,2048]{3,2,1,0:T(8,128)(2,1)} %bitcast.19, bf16[1,768,2048]{2,1,0:T(8,128)(2,1)S(1)} %copy-done), kind=kOutput, calls=%fused_computation.1 | convolution fusion | flops 3623878656 | bytes 11403264 | tf_op jit(solution)/shard_map/dot_general | solution.py:28
  247.2 12.4 %shard_map.282 = (bf16[576,768]{1,0:T(8,128)(2,1)}, bf16[576,768]{1,0:T(8,128)(2,1)}, bf16[576,768]{1,0:T(8,128)(2,1)}, bf16[576,2176]{1,0:T(8,128)(2,1)}) custom-call(s32[1]{0:T(128)} %bitcast.10.who_ref, bf16[576,2176]{1,0:T(8,128)(2,1)} %bitcast.14.refs_5_.x_ref, bf16[2048,768]{1,0:T(8,128)(2,1)} %bitcast.130, bf16[2048,768]{1,0:T(8,128)(2,1)} %bitcast.132, ...), custom_call_target="tpu_custom_call" | custom-call | flops 7247757312 | bytes 20000000 | tf_op jit(solution)/shard_map/pallas_call | solution.py:781
  259.7 10.0 %all-to-all-done.2 = bf16[8,72,2176]{2,1,0:T(8,128)(2,1)} async-done(((bf16[8,72,2176]{2,1,0:T(8,128)(2,1)}), bf16[8,72,2176]{2,1,0:T(8,128)(2,1)}, u32[]{:S(2)}, u32[]{:S(2)}) %all-to-all-start.2) | async-done | bytes 2506784 | tf_op jit(solution)/shard_map/all_to_all | solution.py:1271
  269.7 4.8 all-to-all-start.6
  274.5 12.5 %shard_map.281 = (bf16[576,768]{1,0:T(8,128)(2,1)}, bf16[576,768]{1,0:T(8,128)(2,1)}, bf16[576,768]{1,0:T(8,128)(2,1)}, bf16[576,2176]{1,0:T(8,128)(2,1)}) custom-call(s32[1]{0:T(128)} %bitcast.10.who_ref, bf16[576,2176]{1,0:T(8,128)(2,1)} %bitcast.16.x_ref, bf16[2048,768]{1,0:T(8,128)(2,1)} %bitcast.131, bf16[2048,768]{1,0:T(8,128)(2,1)} %bitcast.133, ...), custom_call_target="tpu_custom_call" | custom-call | flops 7247757312 | bytes 20000000 | tf_op jit(solution)/shard_map/pallas_call | solution.py:781
  287.0 18.0 %all-to-all-done.6 = bf16[8,72,2176]{2,1,0:T(8,128)(2,1)} async-done(((bf16[8,72,2176]{2,1,0:T(8,128)(2,1)}), bf16[8,72,2176]{2,1,0:T(8,128)(2,1)}, u32[]{:S(2)}, u32[]{:S(2)}) %all-to-all-start.6) | async-done | bytes 2506784 | tf_op jit(solution)/shard_map/all_to_all | solution.py:1271
  313.4 4.5 shard_map.285.rest_0_
  317.9 7.8 %fusion.13.rest_1_ = f32[2048,768]{1,0:T(8,128)} fusion(bf16[576,2048]{1,0:T(8,128)(2,1)S(1)} %slice.50, bf16[576,2048]{1,0:T(8,128)(2,1)S(1)} %slice.49, bf16[576,768]{1,0:T(8,128)(2,1)} %get-tuple-element.86, bf16[576,768]{1,0:T(8,128)(2,1)} %get-tuple-element.85), kind=kOutput, calls=%fused_computation.10 | convolution fusion | flops 3636854784 | bytes 12779520 | tf_op jit(solution)/shard_map/dot_general | solution.py:32
  325.7 6.4 fusion.12.rest_2_
  332.1 7.9 %all-to-all-done.5 = bf16[8,72,2176]{2,1,0:T(8,128)(2,1)} async-done(((bf16[8,72,2176]{2,1,0:T(8,128)(2,1)}), bf16[8,72,2176]{2,1,0:T(8,128)(2,1)}, u32[]{:S(2)}, u32[]{:S(2)}) %all-to-all-start.5) | async-done | bytes 2506784 | tf_op jit(solution)/shard_map/all_to_all | solution.py:1271
  339.9 4.5 shard_map.286
  344.5 4.6 fusion.6
  356.6 6.3 fusion.20.refs_8_
  362.9 19.5 %all-to-all-done.4 = bf16[8,72,2048]{2,1,0:T(8,128)(2,1)} async-done(((bf16[8,72,2048]{2,1,0:T(8,128)(2,1)}), bf16[8,72,2048]{2,1,0:T(8,128)(2,1)}, u32[]{:S(2)}, u32[]{:S(2)}) %all-to-all-start.4) | async-done | bytes 2359328 | tf_op jit(solution)/shard_map/all_to_all | solution.py:1271
  382.4 6.0 reduce-scatter.9.cloned.1.call-done.refs_0_
  392.7 4.6 fusion.9
  406.1 24.5 %all-to-all-done.3 = bf16[8,72,2048]{2,1,0:T(8,128)(2,1)} async-done(((bf16[8,72,2048]{2,1,0:T(8,128)(2,1)}), bf16[8,72,2048]{2,1,0:T(8,128)(2,1)}, u32[]{:S(2)}, u32[]{:S(2)}) %all-to-all-start.3) | async-done | bytes 2359328 | tf_op jit(solution)/shard_map/all_to_all | solution.py:1271
  438.2 6.8 %shard_map.289 = (bf16[512,2048]{1,0:T(8,128)(2,1)}, bf16[512,2048]{1,0:T(8,128)(2,1)}) custom-call(s32[1]{0:T(128)} %bitcast.27.d_ref, bf16[512,1024]{1,0:T(8,128)(2,1)} %get-tuple-element.71.a_ref.o_ref, bf16[512,2048]{1,0:T(8,128)(2,1)} %all-gather.5.cloned.1.call-done.rows_ref.b_ref, bf16[512,2048]{1,0:T(8,128)(2,1)} %shard_map.284.rest_0_), custom_call_target="tpu_custom_call" | custom-call | flops 2147483648 | bytes 6000000 | tf_op jit(solution)/shard_map/pallas_call | solution.py:440
  445.0 7.6 %shard_map.288 = (bf16[2,8,256,128]{3,2,1,0:T(8,128)(2,1)}, f32[2,8,8,256]{3,2,1,0:T(8,128)}) custom-call(bf16[512,2048]{1,0:T(8,128)(2,1)} %all-gather.5.cloned.1.call-done.rows_ref.b_ref, bf16[1024,2048]{1,0:T(8,128)(2,1)} %w_ref.3, bf16[512,1024]{1,0:T(8,128)(2,1)} %get-tuple-element.71.a_ref.o_ref, f32[2,8,256,128]{3,2,1,0:T(8,128)} %get-tuple-element.91.inv_ref, ...), custom_call_target="tpu_custom_call" | custom-call | flops 2147483648 | bytes 12000000 | tf_op jit(solution)/shard_map/pallas_call | solution.py:242
  455.9 4.7 all-to-all-start.7
  460.6 28.9 %shard_map.291 = (f32[2048,256]{1,0:T(8,128)}, bf16[512,1024]{1,0:T(8,128)(2,1)}, f32[1,128]{1,0:T(1,128)}) custom-call(s32[2]{0:T(128)} %get-tuple-element.125.qpos_ref, s32[8]{0:T(128)} %select_reduce_fusion.kidx_ref, bf16[2,8,256,128]{3,2,1,0:T(8,128)(2,1)} %get-tuple-element.69.q_ref, bf16[2,8,256,128]{3,2,1,0:T(8,128)(2,1)} %get-tuple-element.92.rest_0_.do_ref, ...), custom_call_target="tpu_custom_call" | custom-call | flops 16106127360 | bytes 12000000 | tf_op jit(solution)/shard_map/pallas_call | solution.py:337
  499.1 6.7 %shard_map.293 = (bf16[1024,1024]{1,0:T(8,128)(2,1)}, bf16[1024,1024]{1,0:T(8,128)(2,1)}) custom-call(s32[1]{0:T(128)} %bitcast.27.d_ref, bf16[512,2048]{1,0:T(8,128)(2,1)} %get-tuple-element.68.x_ref.a_ref.rows_ref, bf16[512,1024]{1,0:T(8,128)(2,1)} %get-tuple-element.97.b_ref.q_ref, bf16[128,2048]{1,0:T(8,128)(2,1)} %shard_map.292.rest_0_.refs_0_.refs_4_), custom_call_target="tpu_custom_call" | custom-call | flops 2147483648 | bytes 6000000 | tf_op jit(solution)/shard_map/pallas_call | solution.py:440
  506.3 4.7 all-to-all-done.8.parts_ref
  513.5 7.3 %shard_map.295 = (bf16[512,2048]{1,0:T(8,128)(2,1)}, f32[1,2048]{1,0:T(1,128)}) custom-call(bf16[512,1024]{1,0:T(8,128)(2,1)} %get-tuple-element.97.b_ref.q_ref, bf16[512,256]{1,0:T(8,128)(2,1)} %get-tuple-element.101.kv_ref.b_ref, bf16[2048,1024]{1,0:T(8,128)(2,1)} %wq_ref.1, bf16[2048,256]{1,0:T(8,128)(2,1)} %constant_dynamic-update-slice_fusion.refs_7_.wkv_ref, ...), custom_call_target="tpu_custom_call" | custom-call | flops 2684354560 | bytes 12000000 | tf_op jit(solution)/shard_map/pallas_call | solution.py:934
  522.9 13.1 %collective-permute-done.17.refs_1_.rest_0_.refs_5_ = bf16[128,2048]{1,0:T(8,128)(2,1)} collective-permute-done((bf16[128,2048]{1,0:T(8,128)(2,1)}, bf16[128,2048]{1,0:T(8,128)(2,1)}, u32[]{:S(2)}, u32[]{:S(2)}) %collective-permute-start.17) | collective-permute-done | bytes 524320 | tf_op jit(solution)/shard_map/ppermute | solution.py:1059
  545.5 5.2 shard_map.301
  557.7 13.5 %collective-permute-done.25.refs_1_ = bf16[512,1280]{1,0:T(8,128)(2,1)} collective-permute-done((bf16[512,1280]{1,0:T(8,128)(2,1)}, bf16[512,1280]{1,0:T(8,128)(2,1)}, u32[]{:S(2)}, u32[]{:S(2)}) %collective-permute-start.25) | collective-permute-done | bytes 1310752 | tf_op jit(solution)/shard_map/ppermute | solution.py:1059
  593.1 4.6 shard_map.298.refs_4_
  597.8 4.7 shard_map.299
  612.8 7.8 %collective-permute-done.30.refs_2_ = bf16[256,1280]{1,0:T(8,128)(2,1)} collective-permute-done((bf16[256,1280]{1,0:T(8,128)(2,1)}, bf16[256,1280]{1,0:T(8,128)(2,1)}, u32[]{:S(2)}, u32[]{:S(2)}) %collective-permute-start.30) | collective-permute-done | bytes 655392 | tf_op jit(solution)/shard_map/ppermute | solution.py:1046
  624.7 5.1 shard_map.304
  629.8 5.1 shard_map.305
  (167 shorter events, 166.3 us)
Async XLA Ops:
  7.2 106.8 %all-gather.3.cloned.1.call-start = ((), (), s32[]{:S(2)}) async-start(), calls=%async_computation.15 | async-start | bytes 2785280 | tf_op jit(solution)/shard_map/all_gather | solution.py:1254
  10.7 17.2 %collective-permute-start.3 = (bf16[128,2048]{1,0:T(8,128)(2,1)}, bf16[128,2048]{1,0:T(8,128)(2,1)}, u32[]{:S(2)}, u32[]{:S(2)}) collective-permute-start(bf16[128,2048]{1,0:T(8,128)(2,1)} %fusion.26.refs_3_), channel_id=1, source_target_pairs={{1,0},{2,1},{3,2},{5,4},{6,5},{7,6},{9,8},{10,9},{11,10},{13,12},{... | collective-permute-start | bytes 1572872 | tf_op jit(solution)/shard_map/ppermute | solution.py:1138
  12.0 17.2 %collective-permute-start = (bf16[128,2048]{1,0:T(8,128)(2,1)}, bf16[128,2048]{1,0:T(8,128)(2,1)}, u32[]{:S(2)}, u32[]{:S(2)}) collective-permute-start(bf16[128,2048]{1,0:T(8,128)(2,1)} %fusion.26.refs_3_), channel_id=1, source_target_pairs={{0,1},{1,2},{2,3},{4,5},{5,6},{6,7},{8,9},{9,10},{10,11},{12,13},{... | collective-permute-start | bytes 1572872 | tf_op jit(solution)/shard_map/ppermute | solution.py:1135
  27.8 15.3 %collective-permute-start.4 = (bf16[128,2048]{1,0:T(8,128)(2,1)}, bf16[128,2048]{1,0:T(8,128)(2,1)}, u32[]{:S(2)}, u32[]{:S(2)}) collective-permute-start(bf16[128,2048]{1,0:T(8,128)(2,1)} %collective-permute-done.3.refs_4_), channel_id=1, source_target_pairs={{1,0},{2,1},{5,4},{6,5},{9,8},{10,9},{13,12},{14,13},{17,16},{18,1... | collective-permute-start | bytes 1572872 | tf_op jit(solution)/shard_map/ppermute | solution.py:1138
  29.1 15.3 %collective-permute-start.1 = (bf16[128,2048]{1,0:T(8,128)(2,1)}, bf16[128,2048]{1,0:T(8,128)(2,1)}, u32[]{:S(2)}, u32[]{:S(2)}) collective-permute-start(bf16[128,2048]{1,0:T(8,128)(2,1)} %collective-permute-done.refs_2_), channel_id=1, source_target_pairs={{1,2},{2,3},{5,6},{6,7},{9,10},{10,11},{13,14},{14,15},{17,18},{18... | collective-permute-start | bytes 1572872 | tf_op jit(solution)/shard_map/ppermute | solution.py:1135
  43.1 14.4 %collective-permute-start.5 = (bf16[128,2048]{1,0:T(8,128)(2,1)}, bf16[128,2048]{1,0:T(8,128)(2,1)}, u32[]{:S(2)}, u32[]{:S(2)}) collective-permute-start(bf16[128,2048]{1,0:T(8,128)(2,1)} %collective-permute-done.4.refs_5_), channel_id=1, source_target_pairs={{1,0},{5,4},{9,8},{13,12},{17,16},{21,20},{25,24},{29,28}} | collective-permute-start | bytes 1572872 | tf_op jit(solution)/shard_map/ppermute | solution.py:1138
  44.4 13.1 %collective-permute-start.2 = (bf16[128,2048]{1,0:T(8,128)(2,1)}, bf16[128,2048]{1,0:T(8,128)(2,1)}, u32[]{:S(2)}, u32[]{:S(2)}) collective-permute-start(bf16[128,2048]{1,0:T(8,128)(2,1)} %collective-permute-done.1.refs_1_), channel_id=1, source_target_pairs={{2,3},{6,7},{10,11},{14,15},{18,19},{22,23},{26,27},{30,31}} | collective-permute-start | bytes 1572872 | tf_op jit(solution)/shard_map/ppermute | solution.py:1135
  62.4 100.5 %reduce-scatter.5.cloned.1.call-start = ((), (), s32[]{:S(2)}) async-start(), calls=%async_computation.16 | async-start | bytes 2621440 | tf_op jit(solution)/shard_map/reduce_scatter | solution.py:1277
  63.6 13.2 %collective-permute-start.8 = (bf16[512,256]{0,1:T(8,128)(2,1)S(1)}, bf16[512,256]{0,1:T(8,128)(2,1)S(1)}, u32[]{:S(2)}, u32[]{:S(2)}) collective-permute-start(bf16[512,256]{0,1:T(8,128)(2,1)S(1)} %copy.59), channel_id=1, source_target_pairs={{0,4},{4,0},{8,12},{12,8},{1,5},{5,1},{9,13},{13,9},{2,6},{6,2},{1... | collective-permute-start | bytes 786440 | tf_op jit(solution)/shard_map/ppermute | solution.py:1147
  64.7 12.2 %collective-permute-start.7 = (bf16[512,256]{0,1:T(8,128)(2,1)S(1)}, bf16[512,256]{0,1:T(8,128)(2,1)S(1)}, u32[]{:S(2)}, u32[]{:S(2)}) collective-permute-start(bf16[512,256]{0,1:T(8,128)(2,1)S(1)} %copy.59), channel_id=1, source_target_pairs={{0,8},{4,12},{8,0},{12,4},{1,9},{5,13},{9,1},{13,5},{2,10},{6,14},... | collective-permute-start | bytes 786440 | tf_op jit(solution)/shard_map/ppermute | solution.py:1147
  66.2 10.6 %collective-permute-start.6 = (bf16[512,256]{0,1:T(8,128)(2,1)S(1)}, bf16[512,256]{0,1:T(8,128)(2,1)S(1)}, u32[]{:S(2)}, u32[]{:S(2)}) collective-permute-start(bf16[512,256]{0,1:T(8,128)(2,1)S(1)} %copy.59), channel_id=1, source_target_pairs={{0,12},{4,8},{8,4},{12,0},{1,13},{5,9},{9,5},{13,1},{2,14},{6,10},... | collective-permute-start | bytes 786440 | tf_op jit(solution)/shard_map/ppermute | solution.py:1147
  128.7 59.0 %all-to-all-start = ((bf16[8,144,2048]{2,1,0:T(8,128)(2,1)}), bf16[8,144,2048]{2,1,0:T(8,128)(2,1)}, u32[]{:S(2)}, u32[]{:S(2)}) async-start(bf16[8,144,2048]{2,1,0:T(8,128)(2,1)} %bitcast.104), calls=%async_computation.1 | async-start | bytes 9437184 | tf_op jit(solution)/shard_map/all_to_all | solution.py:1271
  165.8 21.9 %collective-permute-start.12 = (bf16[128,2176]{1,0:T(8,128)(2,1)}, bf16[128,2176]{1,0:T(8,128)(2,1)}, u32[]{:S(2)}, u32[]{:S(2)}) collective-permute-start(bf16[128,2176]{1,0:T(8,128)(2,1)} %get-tuple-element.77.refs_1_), channel_id=1, source_target_pairs={{1,0},{2,1},{3,2},{5,4},{6,5},{7,6},{9,8},{10,9},{11,10},{13,12},{... | collective-permute-start | bytes 1671176 | tf_op jit(solution)/shard_map/ppermute | solution.py:1138
  167.1 20.6 %collective-permute-start.9 = (bf16[128,2176]{1,0:T(8,128)(2,1)}, bf16[128,2176]{1,0:T(8,128)(2,1)}, u32[]{:S(2)}, u32[]{:S(2)}) collective-permute-start(bf16[128,2176]{1,0:T(8,128)(2,1)} %get-tuple-element.77.refs_1_), channel_id=1, source_target_pairs={{0,1},{1,2},{2,3},{4,5},{5,6},{6,7},{8,9},{9,10},{10,11},{12,13},{... | collective-permute-start | bytes 1671176 | tf_op jit(solution)/shard_map/ppermute | solution.py:1135
  191.6 39.0 %all-to-all-start.1 = ((bf16[8,72,2176]{2,1,0:T(8,128)(2,1)}), bf16[8,72,2176]{2,1,0:T(8,128)(2,1)}, u32[]{:S(2)}, u32[]{:S(2)}) async-start(bf16[8,72,2176]{2,1,0:T(8,128)(2,1)} %bitcast.96), calls=%async_computation.2 | async-start | bytes 5013504 | tf_op jit(solution)/shard_map/all_to_all | solution.py:1271
  196.0 17.0 %collective-permute-start.13 = (bf16[128,2176]{1,0:T(8,128)(2,1)}, bf16[128,2176]{1,0:T(8,128)(2,1)S(1)}, u32[]{:S(2)}, u32[]{:S(2)}) collective-permute-start(bf16[128,2176]{1,0:T(8,128)(2,1)} %collective-permute-done.12.refs_2_), channel_id=1, source_target_pairs={{1,0},{2,1},{5,4},{6,5},{9,8},{10,9},{13,12},{14,13},{17,16},{18,1... | collective-permute-start | bytes 1671176 | tf_op jit(solution)/shard_map/ppermute | solution.py:1138
  197.3 17.8 %collective-permute-start.10 = (bf16[128,2176]{1,0:T(8,128)(2,1)}, bf16[128,2176]{1,0:T(8,128)(2,1)S(1)}, u32[]{:S(2)}, u32[]{:S(2)}) collective-permute-start(bf16[128,2176]{1,0:T(8,128)(2,1)} %collective-permute-done.9.refs_0_), channel_id=1, source_target_pairs={{1,2},{2,3},{5,6},{6,7},{9,10},{10,11},{13,14},{14,15},{17,18},{18... | collective-permute-start | bytes 1671176 | tf_op jit(solution)/shard_map/ppermute | solution.py:1135
  213.8 16.0 %collective-permute-start.14 = (bf16[128,2176]{1,0:T(8,128)(2,1)S(1)}, bf16[128,2176]{1,0:T(8,128)(2,1)S(1)}, u32[]{:S(2)}, u32[]{:S(2)}) collective-permute-start(bf16[128,2176]{1,0:T(8,128)(2,1)S(1)} %collective-permute-done.13.refs_3_), channel_id=1, source_target_pairs={{1,0},{5,4},{9,8},{13,12},{17,16},{21,20},{25,24},{29,28}} | collective-permute-start | bytes 1671176 | tf_op jit(solution)/shard_map/ppermute | solution.py:1138
  215.1 15.5 %collective-permute-start.11 = (bf16[128,2176]{1,0:T(8,128)(2,1)S(1)}, bf16[128,2176]{1,0:T(8,128)(2,1)}, u32[]{:S(2)}, u32[]{:S(2)}) collective-permute-start(bf16[128,2176]{1,0:T(8,128)(2,1)S(1)} %collective-permute-done.10.refs_1_), channel_id=1, source_target_pairs={{2,3},{6,7},{10,11},{14,15},{18,19},{22,23},{26,27},{30,31}} | collective-permute-start | bytes 1671176 | tf_op jit(solution)/shard_map/ppermute | solution.py:1135
  234.8 34.9 %all-to-all-start.2 = ((bf16[8,72,2176]{2,1,0:T(8,128)(2,1)}), bf16[8,72,2176]{2,1,0:T(8,128)(2,1)}, u32[]{:S(2)}, u32[]{:S(2)}) async-start(bf16[8,72,2176]{2,1,0:T(8,128)(2,1)} %bitcast.97), calls=%async_computation.3 | async-start | bytes 5013504 | tf_op jit(solution)/shard_map/all_to_all | solution.py:1271
  269.7 35.3 %all-to-all-start.6 = ((bf16[8,72,2176]{2,1,0:T(8,128)(2,1)}), bf16[8,72,2176]{2,1,0:T(8,128)(2,1)}, u32[]{:S(2)}, u32[]{:S(2)}) async-start(bf16[8,72,2176]{2,1,0:T(8,128)(2,1)} %bitcast.110), calls=%async_computation.8 | async-start | bytes 5013504 | tf_op jit(solution)/shard_map/all_to_all | solution.py:1271
  305.0 34.9 %all-to-all-start.5 = ((bf16[8,72,2176]{2,1,0:T(8,128)(2,1)}), bf16[8,72,2176]{2,1,0:T(8,128)(2,1)}, u32[]{:S(2)}, u32[]{:S(2)}) async-start(bf16[8,72,2176]{2,1,0:T(8,128)(2,1)} %bitcast.109), calls=%async_computation.7 | async-start | bytes 5013504 | tf_op jit(solution)/shard_map/all_to_all | solution.py:1271
  309.4 78.9 %reduce-scatter.9.cloned.1.call-start = ((), (), s32[]{:S(2)}) async-start(), calls=%async_computation.18 | async-start | bytes 2785280 | tf_op jit(solution)/shard_map/reduce_scatter | solution.py:1309
  349.1 33.3 %all-to-all-start.4 = ((bf16[8,72,2048]{2,1,0:T(8,128)(2,1)}), bf16[8,72,2048]{2,1,0:T(8,128)(2,1)}, u32[]{:S(2)}, u32[]{:S(2)}) async-start(bf16[8,72,2048]{2,1,0:T(8,128)(2,1)} %bitcast.111), calls=%async_computation.5 | async-start | bytes 4718592 | tf_op jit(solution)/shard_map/all_to_all | solution.py:1271
  353.4 84.7 %all-gather.5.cloned.1.call-start = ((), (), s32[]{:S(2)}) async-start(), calls=%async_computation.19 | async-start | bytes 2621440 | tf_op jit(solution)/shard_map/all_gather | solution.py:1327
  397.2 33.3 %all-to-all-start.3 = ((bf16[8,72,2048]{2,1,0:T(8,128)(2,1)}), bf16[8,72,2048]{2,1,0:T(8,128)(2,1)}, u32[]{:S(2)}, u32[]{:S(2)}) async-start(bf16[8,72,2048]{2,1,0:T(8,128)(2,1)} %bitcast.112), calls=%async_computation.4 | async-start | bytes 4718592 | tf_op jit(solution)/shard_map/all_to_all | solution.py:1271
  401.6 181.7 %reduce-scatter.7.cloned.1.call-start = ((), (), s32[]{:S(2)}) async-start(), calls=%async_computation.17 | async-start | bytes 2621440 | tf_op jit(solution)/shard_map/reduce_scatter | solution.py:1332
  455.9 36.2 %all-to-all-start.7 = ((bf16[4,128,2048]{2,1,0:T(8,128)(2,1)}), bf16[4,128,2048]{2,1,0:T(8,128)(2,1)}, u32[]{:S(2)}, u32[]{:S(2)}) async-start(bf16[4,128,2048]{2,1,0:T(8,128)(2,1)} %bitcast.98), calls=%async_computation.10 | async-start | bytes 4194304 | tf_op jit(solution)/shard_map/all_to_all | solution.py:1050
  492.1 18.8 %all-to-all-start.8 = ((bf16[4,512,256]{2,1,0:T(8,128)(2,1)}), bf16[4,512,256]{2,1,0:T(8,128)(2,1)}, u32[]{:S(2)}, u32[]{:S(2)}) async-start(bf16[4,512,256]{2,1,0:T(8,128)(2,1)} %bitcast.106), calls=%async_computation.11 | async-start | bytes 2097152 | tf_op jit(solution)/shard_map/all_to_all | solution.py:1050
  496.4 107.2 %reduce-scatter.11.cloned.1.call-start = ((), (), s32[]{:S(2)}) async-start(), calls=%async_computation.20 | async-start | bytes 2621440 | tf_op jit(solution)/shard_map/reduce_scatter | solution.py:1391
  505.8 39.7 %collective-permute-start.23 = (bf16[1024,1024]{1,0:T(8,128)(2,1)}, bf16[1024,1024]{1,0:T(8,128)(2,1)}, u32[]{:S(2)}, u32[]{:S(2)}) collective-permute-start(bf16[1024,1024]{1,0:T(8,128)(2,1)} %get-tuple-element.109), channel_id=1, source_target_pairs={{0,16},{16,0},{1,17},{17,1},{2,18},{18,2},{3,19},{19,3},{4,20},{20... | collective-permute-start | bytes 6291464 | tf_op jit(solution)/shard_map/ppermute | solution.py:1041
  520.9 15.2 %collective-permute-start.17 = (bf16[128,2048]{1,0:T(8,128)(2,1)}, bf16[128,2048]{1,0:T(8,128)(2,1)}, u32[]{:S(2)}, u32[]{:S(2)}) collective-permute-start(bf16[128,2048]{1,0:T(8,128)(2,1)} %shard_map.292.rest_0_.refs_0_.refs_4_), channel_id=1, source_target_pairs={{0,8},{4,12},{8,0},{12,4},{16,20},{20,16},{24,28},{28,24},{1,9},{5... | collective-permute-start | bytes 1572872 | tf_op jit(solution)/shard_map/ppermute | solution.py:1059
  522.4 14.1 %collective-permute-start.19 = (bf16[128,2048]{1,0:T(8,128)(2,1)}, bf16[128,2048]{1,0:T(8,128)(2,1)S(1)}, u32[]{:S(2)}, u32[]{:S(2)}) collective-permute-start(bf16[128,2048]{1,0:T(8,128)(2,1)} %shard_map.292.rest_0_.refs_0_.refs_4_), channel_id=1, source_target_pairs={{0,4},{4,0},{8,12},{12,8},{16,24},{20,28},{24,16},{28,20},{1,5},{5... | collective-permute-start | bytes 1572872 | tf_op jit(solution)/shard_map/ppermute | solution.py:1059
  536.0 9.5 %collective-permute-start.21 = (bf16[128,2048]{1,0:T(8,128)(2,1)}, bf16[128,2048]{1,0:T(8,128)(2,1)}, u32[]{:S(2)}, u32[]{:S(2)}) collective-permute-start(bf16[128,2048]{1,0:T(8,128)(2,1)} %collective-permute-done.17.refs_1_.rest_0_.refs_5_), channel_id=1, source_target_pairs={{0,4},{4,0},{8,12},{12,8},{16,24},{20,28},{24,16},{28,20},{1,5},{5... | collective-permute-start | bytes 1572872 | tf_op jit(solution)/shard_map/ppermute | solution.py:1059
  550.8 20.4 %collective-permute-start.25 = (bf16[512,1280]{1,0:T(8,128)(2,1)}, bf16[512,1280]{1,0:T(8,128)(2,1)}, u32[]{:S(2)}, u32[]{:S(2)}) collective-permute-start(bf16[512,1280]{1,0:T(8,128)(2,1)} %get-tuple-element.113), channel_id=1, source_target_pairs={{0,4},{4,0},{8,12},{12,8},{16,24},{20,28},{24,16},{28,20},{1,5},{5... | collective-permute-start | bytes 3932168 | tf_op jit(solution)/shard_map/ppermute | solution.py:1059
  555.0 24.1 %all-to-all-start.9 = ((bf16[32,2,2048]{2,1,0:T(2,128)(2,1)}), bf16[32,2,2048]{2,1,0:T(2,128)(2,1)S(1)}, u32[]{:S(2)}, u32[]{:S(2)}) async-start(bf16[32,2,2048]{2,1,0:T(2,128)(2,1)} %reshape.167), calls=%async_computation.13 | async-start | bytes 524288 | tf_op jit(solution)/shard_map/all_to_all | solution.py:1386
  575.2 11.1 %collective-permute-start.26 = (bf16[256,1280]{1,0:T(8,128)(2,1)}, bf16[256,1280]{1,0:T(8,128)(2,1)}, u32[]{:S(2)}, u32[]{:S(2)}) collective-permute-start(bf16[256,1280]{1,0:T(8,128)(2,1)} %get-tuple-element.115), channel_id=1, source_target_pairs={{0,8},{4,12},{8,0},{12,4},{16,20},{20,16},{24,28},{28,24},{1,9},{5... | collective-permute-start | bytes 1966088 | tf_op jit(solution)/shard_map/ppermute | solution.py:1059
  576.1 14.6 %collective-permute-start.16 = (bf16[128,2048]{1,0:T(8,128)(2,1)}, bf16[128,2048]{1,0:T(8,128)(2,1)}, u32[]{:S(2)}, u32[]{:S(2)}) collective-permute-start(bf16[128,2048]{1,0:T(8,128)(2,1)} %shard_map.292.rest_0_.refs_0_.refs_4_), channel_id=1, source_target_pairs={{0,16},{16,0},{1,17},{17,1},{2,18},{18,2},{3,19},{19,3},{4,20},{20... | collective-permute-start | bytes 1572872 | tf_op jit(solution)/shard_map/ppermute | solution.py:1041
  576.1 15.2 %collective-permute-start.20 = (bf16[128,2048]{1,0:T(8,128)(2,1)}, bf16[128,2048]{1,0:T(8,128)(2,1)}, u32[]{:S(2)}, u32[]{:S(2)}) collective-permute-start(bf16[128,2048]{1,0:T(8,128)(2,1)} %copy-done.1), channel_id=1, source_target_pairs={{0,16},{16,0},{1,17},{17,1},{2,18},{18,2},{3,19},{19,3},{4,20},{20... | collective-permute-start | bytes 1572872 | tf_op jit(solution)/shard_map/ppermute | solution.py:1041
  580.2 28.9 %all-to-all-start.10 = ((bf16[32,2,2048]{2,1,0:T(2,128)(2,1)}), bf16[32,2,2048]{2,1,0:T(2,128)(2,1)S(1)}, u32[]{:S(2)}, u32[]{:S(2)}) async-start(bf16[32,2,2048]{2,1,0:T(2,128)(2,1)} %broadcast_in_dim.85), calls=%async_computation.14 | async-start | bytes 524288 | tf_op jit(solution)/shard_map/all_to_all | solution.py:1386
  582.8 15.0 %collective-permute-start.18 = (bf16[128,2048]{1,0:T(8,128)(2,1)}, bf16[128,2048]{1,0:T(8,128)(2,1)}, u32[]{:S(2)}, u32[]{:S(2)}) collective-permute-start(bf16[128,2048]{1,0:T(8,128)(2,1)} %collective-permute-done.17.refs_1_.rest_0_.refs_5_), channel_id=1, source_target_pairs={{0,16},{16,0},{1,17},{17,1},{2,18},{18,2},{3,19},{19,3},{4,20},{20... | collective-permute-start | bytes 1572872 | tf_op jit(solution)/shard_map/ppermute | solution.py:1041
  583.0 14.8 %collective-permute-start.22 = (bf16[128,2048]{1,0:T(8,128)(2,1)}, bf16[128,2048]{1,0:T(8,128)(2,1)}, u32[]{:S(2)}, u32[]{:S(2)}) collective-permute-start(bf16[128,2048]{1,0:T(8,128)(2,1)} %collective-permute-done.21.refs_3_.refs_7_), channel_id=1, source_target_pairs={{0,16},{16,0},{1,17},{17,1},{2,18},{18,2},{3,19},{19,3},{4,20},{20... | collective-permute-start | bytes 1572872 | tf_op jit(solution)/shard_map/ppermute | solution.py:1041
  588.4 23.8 %collective-permute-start.32 = (bf16[256,1280]{1,0:T(8,128)(2,1)}, bf16[256,1280]{1,0:T(8,128)(2,1)}, u32[]{:S(2)}, u32[]{:S(2)}) collective-permute-start(bf16[256,1280]{1,0:T(8,128)(2,1)} %shard_map.303.refs_0_), channel_id=1, source_target_pairs={{0,12},{4,8},{8,4},{12,0},{1,13},{5,9},{9,5},{13,1},{2,14},{6,10},... | collective-permute-start | bytes 1966088 | tf_op jit(solution)/shard_map/ppermute | solution.py:1046
  590.7 29.8 %collective-permute-start.30 = (bf16[256,1280]{1,0:T(8,128)(2,1)}, bf16[256,1280]{1,0:T(8,128)(2,1)}, u32[]{:S(2)}, u32[]{:S(2)}) collective-permute-start(bf16[256,1280]{1,0:T(8,128)(2,1)} %shard_map.303.refs_0_), channel_id=1, source_target_pairs={{0,8},{4,12},{8,0},{12,4},{1,9},{5,13},{9,1},{13,5},{2,10},{6,14},... | collective-permute-start | bytes 1966088 | tf_op jit(solution)/shard_map/ppermute | solution.py:1046
  591.3 29.4 %collective-permute-start.28 = (bf16[256,1280]{1,0:T(8,128)(2,1)}, bf16[256,1280]{1,0:T(8,128)(2,1)}, u32[]{:S(2)}, u32[]{:S(2)}) collective-permute-start(bf16[256,1280]{1,0:T(8,128)(2,1)} %shard_map.303.refs_0_), channel_id=1, source_target_pairs={{0,4},{4,0},{8,12},{12,8},{1,5},{5,1},{9,13},{13,9},{2,6},{6,2},{1... | collective-permute-start | bytes 1966088 | tf_op jit(solution)/shard_map/ppermute | solution.py:1046
  603.6 26.1 %collective-permute-start.27 = (bf16[256,1280]{1,0:T(8,128)(2,1)}, bf16[256,1280]{1,0:T(8,128)(2,1)}, u32[]{:S(2)}, u32[]{:S(2)}) collective-permute-start(bf16[256,1280]{1,0:T(8,128)(2,1)} %shard_map.303.refs_0_), channel_id=1, source_target_pairs={{0,16},{16,0},{1,17},{17,1},{2,18},{18,2},{3,19},{19,3},{4,20},{20... | collective-permute-start | bytes 1966088 | tf_op jit(solution)/shard_map/ppermute | solution.py:1041
  612.3 17.5 %collective-permute-start.33 = (bf16[256,1280]{1,0:T(8,128)(2,1)}, bf16[256,1280]{1,0:T(8,128)(2,1)}, u32[]{:S(2)}, u32[]{:S(2)}) collective-permute-start(bf16[256,1280]{1,0:T(8,128)(2,1)} %collective-permute-done.32.refs_3_), channel_id=1, source_target_pairs={{0,16},{16,0},{1,17},{17,1},{2,18},{18,2},{3,19},{19,3},{4,20},{20... | collective-permute-start | bytes 1966088 | tf_op jit(solution)/shard_map/ppermute | solution.py:1041
  620.5 9.2 %collective-permute-start.31 = (bf16[256,1280]{1,0:T(8,128)(2,1)}, bf16[256,1280]{1,0:T(8,128)(2,1)}, u32[]{:S(2)}, u32[]{:S(2)}) collective-permute-start(bf16[256,1280]{1,0:T(8,128)(2,1)} %collective-permute-done.30.refs_2_), channel_id=1, source_target_pairs={{0,16},{16,0},{1,17},{17,1},{2,18},{18,2},{3,19},{19,3},{4,20},{20... | collective-permute-start | bytes 1966088 | tf_op jit(solution)/shard_map/ppermute | solution.py:1041
  (15 other events, 308.5 us)
Sparse Core Ops, SparseCore 0:
  62.6 51.3 all-gather.2
  120.1 42.7 reduce-scatter.4
  344.6 43.7 reduce-scatter.8
  392.8 45.3 all-gather.4
  445.1 42.7 reduce-scatter.6
  521.0 41.4 reduce-scatter.10
where the time goes:
time: 655 us; the launch traced here: 642 us
  waiting for transfers between devices  248 us (38%)
  Pallas kernels  205 us (31%)
  starting transfers between devices  83.6 us (13%)
  matrix products  37.6 us (6%)
  local copies, waits for them, and re-layouts  32.6 us (5%)
  other arithmetic  18.1 us (3%)
  between operations  17 us (3%)
    all_to_all x7, waiting for transfers between devices, swap_plane(): lax.all_to_all(parts, GROUP_AXES, split_axis=0, concat_axis=0, tiled=True)  92.6 us
    ppermute x6, waiting for transfers between devices, line_steps(): lax.ppermute(found[s - 1], 'expert', [(i + 1, i) for i in range(n - s)])  53.3 us
    all_to_all x7, starting transfers between devices, swap_plane(): lax.all_to_all(parts, GROUP_AXES, split_axis=0, concat_axis=0, tiled=True)  31.6 us
    ppermute x5, waiting for transfers between devices, swap(): return lambda rows: lax.ppermute(rows, GROUP_AXES, perm)  30.7 us
    pallas_call x1, Pallas kernels, attend_back(): pl.pallas_call(attend_back_kernel, grid_spec=pltpu.PrefetchScalarGridSpec...  28.9 us
    reduce_scatter x1, waiting for transfers between devices, on_device(): lax.psum_scatter(attn_part, 'expert', scatter_dimension=0, tiled=True)  27.5 us
    pallas_call x2, Pallas kernels, run_expert(): pl.pallas_call(functools.partial(expert_kernel, experts), grid_spec=pltpu...  24.9 us
    all_gather x1, waiting for transfers between devices, on_device(): grad_col = lax.all_gather(grad_wide, 'expert', axis=0, tiled=True)  22 us
  transfers between devices with their start and end apart: 51, of which 22 were waited for; matrix products, arithmetic and copies ran while one was open for 13% of the time, Pallas kernels for 26%

commit v1 on v0

--- a/solution.py
+++ b/solution.py
@@ -55,7 +55,7 @@
     return grad, jnp.sum(g * n, axis=0, keepdims=True)
 
 
-def query_kernel(x_ref, w_ref, gain_ref, cos_ref, sin_ref, rot_ref, proj_ref):
+def query_kernel(x_ref, w_ref, gain_ref, cos_ref, sin_ref, rot_ref, turned_ref, proj_ref):
     tiles, heads, rows, size = rot_ref.shape
     acc = dot_nn(x_ref[...], w_ref[...])
     for h in range(heads):
@@ -63,6 +63,8 @@
         rot = head_forward(u, gain_ref[...], cos_ref[...], sin_ref[...])
         proj_ref[:, h] = u.reshape(tiles, rows, size)
         rot_ref[:, h] = rot.astype(LOW).reshape(tiles, rows, size)
+        for t in range(tiles):
+            turned_ref[t, h] = jnp.transpose(rot[t * rows : (t + 1) * rows]).astype(LOW)
 
 
 def project_queries(normed, weight, gain, cos2, sin2):
@@ -83,8 +85,16 @@
             pl.BlockSpec((block, size), whole),
             pl.BlockSpec((block, size), whole),
         ],
-        out_specs=[pl.BlockSpec((tiles, 2, TILE, size), per)] * 2,
-        out_shape=[jax.ShapeDtypeStruct(shape, LOW), jax.ShapeDtypeStruct(shape, F32)],
+        out_specs=[
+            pl.BlockSpec((tiles, 2, TILE, size), per),
+            pl.BlockSpec((tiles, 2, size, TILE), per),
+            pl.BlockSpec((tiles, 2, TILE, size), per),
+        ],
+        out_shape=[
+            jax.ShapeDtypeStruct(shape, LOW),
+            jax.ShapeDtypeStruct((tiles, heads, size, TILE), LOW),
+            jax.ShapeDtypeStruct(shape, F32),
+        ],
         compiler_params=params(),
         cost_estimate=cost(2 * block * width * heads * size, 12e6),
     )(normed, weight, gain[None], cos2, sin2)
@@ -164,7 +174,7 @@
         step([last], True)
 
 
-def attend_kernel(qpos_ref, kidx_ref, q_ref, kv_ref, *rest):
+def attend_kernel(qpos_ref, kidx_ref, q_ref, kv_ref, kt_ref, *rest):
     out_ref, inv_ref, acc_ref = rest[-3:]
     heads, rows, size = q_ref.shape[1:]
     acc_ref[...] = jnp.zeros_like(acc_ref)
@@ -172,13 +182,13 @@
     def step(places, masked):
         starts = [pl.multiple_of(kidx_ref[place] * rows, rows) for place in places]
         count = len(places) * rows
-        keys = jnp.concatenate([kv_ref[pl.ds(start, rows), :size] for start in starts], axis=0)
+        keys_t = jnp.concatenate([kt_ref[:, pl.ds(start, rows)] for start in starts], axis=1)
         values = jnp.concatenate([kv_ref[pl.ds(start, rows), size:] for start in starts], axis=0)
         values = jnp.concatenate([values, jnp.ones((count, size), LOW)], axis=1)
         for h in range(heads):
             for first in range(0, rows, PIECE):
                 part = slice(first, first + PIECE)
-                e = jnp.exp2(dot_nt(q_ref[0, h, part], keys))
+                e = jnp.exp2(dot_nn(q_ref[0, h, part], keys_t))
                 if masked:
                     qi = lax.broadcasted_iota(jnp.int32, e.shape, 0) + first
                     ki = lax.broadcasted_iota(jnp.int32, e.shape, 1) - (count - rows)
@@ -192,7 +202,7 @@
         out_ref[:, h * size : (h + 1) * size] = (acc_ref[h, :, :size] * inv).astype(LOW)
 
 
-def attend(qpos, kidx, queries, kv, others):
+def attend(qpos, kidx, queries, kv, keys_t, others):
     tiles, heads, rows, size = queries.shape
     seq = kv.shape[0]
     return pl.pallas_call(
@@ -203,6 +213,7 @@
             in_specs=[
                 pl.BlockSpec((1, heads, rows, size), lambda i, a, b: (i, 0, 0, 0)),
                 pl.BlockSpec((seq, 2 * size), lambda i, a, b: (0, 0)),
+                pl.BlockSpec((size, seq), lambda i, a, b: (0, 0)),
             ]
             + [pl.BlockSpec(memory_space=pl.ANY)] * len(others),
             out_specs=[
@@ -219,18 +230,20 @@
         cost_estimate=cost(
             6 * tiles * rows * heads * seq * size, 8e6, tiles * rows * heads * seq
         ),
-    )(qpos, kidx, queries, kv, *others)
+    )(qpos, kidx, queries, kv, keys_t, *others)
 
 
 def grad_out_kernel(rows_ref, w_ref, o_ref, inv_ref, *rest):
-    do_ref, centre_ref = rest[-2:]
+    do_ref, turned_ref, centre_ref = rest[-3:]
     tiles, heads, rows, size = do_ref.shape
     acc = dot_nt(rows_ref[...], w_ref[...])
     for t in range(tiles):
         for h in range(heads):
             part = slice(t * rows, (t + 1) * rows), slice(h * size, (h + 1) * size)
-            low = (acc[part] * inv_ref[t, h]).astype(LOW)
+            scaled = acc[part] * inv_ref[t, h]
+            low = scaled.astype(LOW)
             do_ref[t, h] = low
+            turned_ref[t, h] = jnp.transpose(scaled).astype(LOW)
             product = low.astype(F32) * o_ref[part].astype(F32)
             centre = jnp.sum(jnp.transpose(product), axis=0, keepdims=True)
             centre_ref[t, h] = jnp.broadcast_to(centre, (8, rows))
@@ -251,10 +264,12 @@
         + [pl.BlockSpec(memory_space=pl.ANY)] * len(others),
         out_specs=[
             pl.BlockSpec((tiles, 2, rows, size), lambda i: (0, i, 0, 0)),
+            pl.BlockSpec((tiles, 2, size, rows), lambda i: (0, i, 0, 0)),
             pl.BlockSpec((tiles, 2, 8, rows), lambda i: (0, i, 0, 0)),
         ],
         out_shape=[
             jax.ShapeDtypeStruct((tiles, heads, rows, size), LOW),
+            jax.ShapeDtypeStruct((tiles, heads, size, rows), LOW),
             jax.ShapeDtypeStruct((tiles, heads, 8, rows), F32),
         ],
         compiler_params=params(),
@@ -266,7 +281,9 @@
     qpos_ref,
     kidx_ref,
     q_ref,
+    qt_ref,
     do_ref,
+    dot_ref,
     centre_ref,
     kv_ref,
     kt_ref,
@@ -293,17 +310,17 @@
         values = jnp.concatenate([kv_ref[pl.ds(start, rows), size:] for start in starts], axis=0)
         keys_t = jnp.concatenate([kt_ref[:, pl.ds(start, rows)] for start in starts], axis=1)
         for h in range(heads):
-            query, grad = q_ref[0, h], do_ref[0, h]
+            query_t, grad_t = qt_ref[0, h], dot_ref[0, h]
             centre = centre_ref[0, h, 0:1]
             columns = slice(h * rows, (h + 1) * rows)
             for first in range(0, count, PIECE):
                 part = slice(first, first + PIECE)
-                e = jnp.exp2(dot_nt(keys[part], query))
+                e = jnp.exp2(dot_nn(keys[part], query_t))
                 if masked and first >= count - rows:
                     ki = lax.broadcasted_iota(jnp.int32, e.shape, 0) + (first - (count - rows))
                     qi = lax.broadcasted_iota(jnp.int32, e.shape, 1)
                     e = jnp.where(ki <= qi, e, 0.0)
-                ds = e * (dot_nt(values[part], grad) - centre)
+                ds = e * (dot_nn(values[part], grad_t) - centre)
                 e_ref[part, columns] = e.astype(LOW)
                 ds_ref[part, columns] = ds.astype(LOW)
             acc_ref[h] += dot_nn(keys_t, ds_ref[:count, columns])
@@ -328,10 +345,13 @@
     dgain_ref[...] += total
 
 
-def attend_back(qpos, kidx, queries, grads, centre, kv, keys_t, proj, gain, cos2, sin2, others):
+def attend_back(
+    qpos, kidx, queries, queries_t, grads, grads_t, centre, kv, keys_t, proj, gain, cos2, sin2, others
+):
     tiles, heads, rows, size = queries.shape
     seq = kv.shape[0]
     per = pl.BlockSpec((1, heads, rows, size), lambda i, a, b: (i, 0, 0, 0))
+    turned = pl.BlockSpec((1, heads, size, rows), lambda i, a, b: (i, 0, 0, 0))
     flat = lambda i, a, b: (0, 0)
     rowwise = lambda i, a, b: (i, 0)
     return pl.pallas_call(
@@ -341,7 +361,9 @@
             grid=(tiles,),
             in_specs=[
                 per,
+                turned,
                 per,
+                turned,
                 pl.BlockSpec((1, heads, 8, rows), lambda i, a, b: (i, 0, 0, 0)),
                 pl.BlockSpec((seq, 2 * size), flat),
                 pl.BlockSpec((size, seq), flat),
@@ -368,7 +390,22 @@
         cost_estimate=cost(
             15 * tiles * rows * heads * seq * size, 12e6, tiles * rows * heads * seq
         ),
-    )(qpos, kidx, queries, grads, centre, kv, keys_t, proj, gain[None], cos2, sin2, *others)
+    )(
+        qpos,
+        kidx,
+        queries,
+        queries_t,
+        grads,
+        grads_t,
+        centre,
+        kv,
+        keys_t,
+        proj,
+        gain[None],
+        cos2,
+        sin2,
+        *others,
+    )
 
 
 def out_kernel(a_ref, b_ref, *rest):
@@ -1018,7 +1055,7 @@
                 first += wide
 
 
-def widen(places, chunks, widths, total, into, others):
+def widen(places, chunks, widths, total, others):
     rows, columns = chunks[0].shape
     count = len(chunks)
     return pl.pallas_call(
@@ -1027,14 +1064,13 @@
             num_scalar_prefetch=1,
             grid=(count,),
             in_specs=[full(chunk.shape) for chunk in chunks]
-            + [pl.BlockSpec(memory_space=pl.ANY)] * (len(into) + len(others)),
+            + [pl.BlockSpec(memory_space=pl.ANY)] * len(others),
             out_specs=[pl.BlockSpec((rows, wide), lambda i, at: (at[i], 0)) for wide in widths],
         ),
         out_shape=[jax.ShapeDtypeStruct((total, wide), F32) for wide in widths],
-        input_output_aliases={1 + count + k: k for k in range(len(into))},
         compiler_params=params(),
         cost_estimate=cost(rows * columns, 6 * count * rows * columns),
-    )(jnp.stack(places).astype(jnp.int32), *chunks, *into, *others)
+    )(jnp.stack(places).astype(jnp.int32), *chunks, *others)
 
 
 def swap_dp(rows):
@@ -1101,9 +1137,8 @@
 def widen_all(quarters, places, widths, others):
     count = len(quarters)
     total = 2 * count * quarters[0].shape[0]
-    swapped = [swap_dp(part) for part in quarters]
-    here = widen(places[:count], quarters, widths, total, [], [])
-    return widen(places[count:], swapped, widths, total, here, others)
+    chunks = quarters + [swap_dp(part) for part in quarters]
+    return widen(places, chunks, widths, total, others)
 
 
 def arrival_order(n):
@@ -1253,7 +1288,7 @@
     )
     grad_col = lax.all_gather(grad_wide, "expert", axis=0, tiled=True)
     kv_whole = context_gather(own_kv)
-    queries, query_proj = project_queries(normed_rows, query_weight, q_gain, cos2, sin2)
+    queries, queries_t, query_proj = project_queries(normed_rows, query_weight, q_gain, cos2, sin2)
 
     n_half = n_expert // 2
     order_here = jnp.asarray(arrival_order(n_expert), jnp.int32)[place]
@@ -1271,8 +1306,8 @@
         parts = lax.all_to_all(parts, GROUP_AXES, split_axis=0, concat_axis=0, tiled=True)
         return parts.reshape(rows.shape)
 
-    attended, inverse = attend(qpos, kidx, queries, kv_whole, [])
     keys_t = kv_whole[:, :size].T
+    attended, inverse = attend(qpos, kidx, queries, kv_whole, keys_t, [])
     attn_part = out_dot(attended, output_weight, [grad_col])
     attn_rows = lax.psum_scatter(attn_part, "expert", scatter_dimension=0, tiled=True)
 
@@ -1280,7 +1315,7 @@
     act_pull = dot_nt(grad_x, w_down[0]).reshape(n_groups, 2, n_half * capacity, -1)
 
     hidden, mixed, probs = route_rows(
-        x_low, attn_rows, mlp_gain, router_rows, mask_wide, experts, [keys_t]
+        x_low, attn_rows, mlp_gain, router_rows, mask_wide, experts, []
     )
 
     who = (lax.axis_index(ALL_AXES) * exp_dev).astype(jnp.int32)[None]
@@ -1325,7 +1360,7 @@
 
     returned_far = swap_plane(returned[1])
     grad_attn = lax.all_gather(grad_hidden_low, "expert", axis=0, tiled=True)
-    grad_o, centre = grad_attended(
+    grad_o, grad_o_t, centre = grad_attended(
         grad_attn, output_weight, attended, inverse, [returned_far]
     )
     combined = combine_rows(meta, back_tables, [returned_near, returned_far], n_half, [])
@@ -1337,7 +1372,9 @@
         qpos,
         kidx,
         queries,
+        queries_t,
         grad_o,
+        grad_o_t,
         centre,
         kv_whole,
         keys_t,
@@ -1360,13 +1397,13 @@
     pairs = [(w_query_keep, w_query_got)]
     widths = [query_weight.shape[1]]
     if group_dev == 1:
-        w_kv_send, w_kv_keep = token_halves(normed_rows, kv_grads, w_out_quarters[1:3])
+        w_kv_send, w_kv_keep = token_halves(normed_rows, kv_grads, [])
         pairs.append((w_kv_keep, swap_dp(w_kv_send)))
         widths += [key_weight.shape[1], value_weight.shape[1]]
     grad_normed, gain_rows = normed_back(
         grad_q, kv_grads, query_weight, kv_weights, normed_rows, []
     )
-    send, keep = plane_first(pairs, [*w_out_quarters, grad_normed])
+    send, keep = plane_first(pairs, [grad_normed])
     (grad_w_out,) = widen_all(
         w_out_quarters,
         quarter_places(lambda core, b1, b2: jnp.where(core == 0, b1 + 2 * b2, 2 * b1 + b2)),
@@ -1386,16 +1423,14 @@
     swap_all = lambda rows: lax.all_to_all(rows, ALL_AXES, split_axis=0, concat_axis=0, tiled=True)
     small_parts = swap_all(small.reshape(lax.axis_size(ALL_AXES), -1, width))
     small_own = jnp.sum(small_parts.astype(F32), axis=0).astype(LOW)
-    second_send, second_keep = plane_second(send, keep, [small])
+    second_send, second_keep = plane_second(send, keep, [small, *w_out_quarters[1:3]])
     quarter = plane_last(second_send, second_keep, [output_rows, small_own])
     grad_normed = lax.psum_scatter(grad_normed, "expert", scatter_dimension=0, tiled=True)
     grad_input = input_back(grad_normed, x_low, attn_gain, grad_hidden)
     small_sum = swap_all(jnp.broadcast_to(small_own[None], small_parts.shape))
     small_sum = small_sum.reshape(small.shape).astype(F32) + zero_of(grad_w_out, grad_input)
-    quarters = [quarter] + [swap_context(quarter, s) for s in range(1, n_context)]
-    d = lax.axis_index("dp")
-    turned = lambda core, c: jnp.where(core == 0, 2 * lax.rem(c, 2) + lax.div(c, 2), c)
-    places = [4 * core + turned(core, context ^ s) for core in (d, 1 - d) for s in range(n_context)]
+    quarters = plane_spread(quarter)
+    places = quarter_places(lambda core, b1, b2: 2 * b1 + b2)
     grad_w_query, *more = widen_all(quarters, places, widths, [small_sum])
     if group_dev == 1:
         grad_w_key, grad_w_value = more

time: 655 us -> 654 us (level)
  Pallas kernels: 205 us -> 198 us
    ppermute x6, waiting for transfers between devices: 0.02 us -> 8.35 us  [line_steps(): lax.ppermute(found[1 - s], 'expert', [(i, i + 1) for i in range(s - 1, n...]
    ppermute x3 -> x0, waiting for transfers between devices: 7.91 us -> none  [swap_context(): return lax.ppermute(rows, 'context', [(i, i ^ s) for i in range(n)])]
    pallas_call x4 -> x2, Pallas kernels: 19.5 us -> 15.6 us  [widen(): pl.pallas_call(functools.partial(widen_kernel, count, len(widths)), grid_...]
    ppermute x5 -> x8, waiting for transfers between devices: 30.7 us -> 32.6 us  [swap(): return lambda rows: lax.ppermute(rows, GROUP_AXES, perm)]
  transfers between devices with their start and end apart: 51 -> 51, of which waited for: 22 -> 23; matrix products, arithmetic and copies ran while one was open for 13% -> 13% of each run, Pallas kernels for 26% -> 24%
where the time goes in v1:
time: 654 us; the launch traced here: 641 us
  waiting for transfers between devices  253 us (39%)
  Pallas kernels  198 us (30%)
  starting transfers between devices  84.1 us (13%)
  matrix products  37.6 us (6%)
  local copies, waits for them, and re-layouts  33.6 us (5%)
  other arithmetic  17 us (3%)
  between operations  17 us (3%)
    all_to_all x7, waiting for transfers between devices, swap_plane(): lax.all_to_all(parts, GROUP_AXES, split_axis=0, concat_axis=0, tiled=True)  95.9 us
    ppermute x6, waiting for transfers between devices, line_steps(): lax.ppermute(found[s - 1], 'expert', [(i + 1, i) for i in range(n - s)])  50 us
    ppermute x8, waiting for transfers between devices, swap(): return lambda rows: lax.ppermute(rows, GROUP_AXES, perm)  32.6 us
    all_to_all x7, starting transfers between devices, swap_plane(): lax.all_to_all(parts, GROUP_AXES, split_axis=0, concat_axis=0, tiled=True)  31.5 us
    reduce_scatter x1, waiting for transfers between devices, on_device(): lax.psum_scatter(attn_part, 'expert', scatter_dimension=0, tiled=True)  29.3 us
    pallas_call x1, Pallas kernels, attend_back(): pl.pallas_call(attend_back_kernel, grid_spec=pltpu.PrefetchScalarGridSpec...  25.7 us
    pallas_call x2, Pallas kernels, run_expert(): pl.pallas_call(functools.partial(expert_kernel, experts), grid_spec=pltpu...  24.9 us
    dot_general x3, matrix products, dot_tn(): lax.dot_general(a, b, (((0,), (0,)), ((), ())), preferred_element_type=F32)  20.4 us
  transfers between devices with their start and end apart: 51, of which 23 were waited for; matrix products, arithmetic and copies ran while one was open for 13% of the time, Pallas kernels for 24%

profile of v1, /device:TPU:0, one launch (start us, length us, event | category | flops | bytes accessed | tf_op | source)
XLA Modules:
  0.0 640.8 jit_solution(11770430014768890786)
XLA Ops:
  10.7 5.7 collective-permute-start
  18.7 8.3 %collective-permute-done.refs_2_ = bf16[128,2048]{1,0:T(8,128)(2,1)} collective-permute-done((bf16[128,2048]{1,0:T(8,128)(2,1)}, bf16[128,2048]{1,0:T(8,128)(2,1)}, u32[]{:S(2)}, u32[]{:S(2)}) %collective-permute-start) | collective-permute-done | bytes 524320 | tf_op jit(solution)/shard_map/ppermute | solution.py:1170
  37.9 8.9 %collective-permute-done.4.refs_5_ = bf16[128,2048]{1,0:T(8,128)(2,1)} collective-permute-done((bf16[128,2048]{1,0:T(8,128)(2,1)}, bf16[128,2048]{1,0:T(8,128)(2,1)}, u32[]{:S(2)}, u32[]{:S(2)}) %collective-permute-start.4) | collective-permute-done | bytes 524320 | tf_op jit(solution)/shard_map/ppermute | solution.py:1173
  52.4 8.3 %collective-permute-done.5.refs_6_ = bf16[128,2048]{1,0:T(8,128)(2,1)} collective-permute-done((bf16[128,2048]{1,0:T(8,128)(2,1)}, bf16[128,2048]{1,0:T(8,128)(2,1)}, u32[]{:S(2)}, u32[]{:S(2)}) %collective-permute-start.5) | collective-permute-done | bytes 524320 | tf_op jit(solution)/shard_map/ppermute | solution.py:1173
  60.8 4.9 shard_map.272
  71.0 9.6 %shard_map.273 = (bf16[2,8,256,128]{3,2,1,0:T(8,128)(2,1)}, bf16[2,8,128,256]{3,2,1,0:T(8,128)(2,1)}, f32[2,8,256,128]{3,2,1,0:T(8,128)}) custom-call(bf16[512,2048]{1,0:T(8,128)(2,1)} %get-tuple-element.67.x_ref.a_ref.rows_ref, bf16[2048,1024]{1,0:T(8,128)(2,1)} %wq_ref.1, f32[1,128]{1,0:T(1,128)} %bitcast.134, ...), custom_call_target="tpu_custom_call" | custom-call | flops 2147483648 | bytes 12000000 | tf_op jit(solution)/shard_map/pallas_call | solution.py:78
  86.0 10.8 %shard_map.274 = (bf16[512,1024]{1,0:T(8,128)(2,1)}, f32[2,8,256,128]{3,2,1,0:T(8,128)}) custom-call(s32[2]{0:T(128)} %get-tuple-element.123.qpos_ref, s32[8]{0:T(128)} %select_reduce_fusion.kidx_ref, bf16[2,8,256,128]{3,2,1,0:T(8,128)(2,1)} %get-tuple-element.68.q_ref, bf16[2048,256]{1,0:T(8,128)(2,1)} %copy.62.kv_ref, ...), custom_call_target="tpu_custom_call" | custom-call | flops 6442450944 | bytes 8000000 | tf_op jit(solution)/shard_map/pallas_call | solution.py:208
  96.8 15.5 %all-gather.3.cloned.1.call-done.rest_0_.col_ref = bf16[512,2176]{1,0:T(8,128)(2,1)} async-done(((bf16[128,2176]{1,0:T(8,128)(2,1)}), bf16[512,2176]{1,0:T(8,128)(2,1)}) %all-gather.3.cloned.1.call-update) | async-done | bytes 2228240 | tf_op jit(solution)/shard_map/all_gather | solution.py:1289
  112.3 6.0 shard_map.275
  119.8 7.3 %shard_map.277 = (bf16[1152,2048]{1,0:T(8,128)(2,1)}, f32[8,512]{1,0:T(8,128)}) custom-call(s32[9]{0:T(128)} %pad_add_fusion.meta_ref, bf16[512,2176]{1,0:T(8,128)(2,1)} %all-gather.3.cloned.1.call-done.rest_0_.col_ref), custom_call_target="tpu_custom_call" | custom-call | flops 2415919104 | bytes 8000000 | tf_op jit(solution)/shard_map/pallas_call | solution.py:609
  127.1 4.8 all-to-all-start
  131.9 29.3 %reduce-scatter.5.cloned.1.call-done.refs_1_ = bf16[128,2048]{1,0:T(8,128)(2,1)} async-done(((bf16[512,2048]{1,0:T(8,128)(2,1)}), bf16[128,2048]{1,0:T(8,128)(2,1)}) %reduce-scatter.5.cloned.1.call-update) | async-done | bytes 524304 | tf_op jit(solution)/shard_map/reduce_scatter | solution.py:1312
  170.1 16.0 %all-to-all-done = bf16[8,144,2048]{2,1,0:T(8,128)(2,1)} async-done(((bf16[8,144,2048]{2,1,0:T(8,128)(2,1)}), bf16[8,144,2048]{2,1,0:T(8,128)(2,1)}, u32[]{:S(2)}, u32[]{:S(2)}) %all-to-all-start) | async-done | bytes 4718624 | tf_op jit(solution)/shard_map/all_to_all | solution.py:1306
  197.9 15.3 %collective-permute-done.13.refs_3_ = bf16[128,2176]{1,0:T(8,128)(2,1)S(1)} collective-permute-done((bf16[128,2176]{1,0:T(8,128)(2,1)}, bf16[128,2176]{1,0:T(8,128)(2,1)S(1)}, u32[]{:S(2)}, u32[]{:S(2)}) %collective-permute-start.13) | collective-permute-done | bytes 557088 | tf_op jit(solution)/shard_map/ppermute | solution.py:1173
  215.3 14.1 %collective-permute-done.14.refs_4_ = bf16[128,2176]{1,0:T(8,128)(2,1)} collective-permute-done((bf16[128,2176]{1,0:T(8,128)(2,1)S(1)}, bf16[128,2176]{1,0:T(8,128)(2,1)}, u32[]{:S(2)}, u32[]{:S(2)}) %collective-permute-start.14) | collective-permute-done | bytes 557088 | tf_op jit(solution)/shard_map/ppermute | solution.py:1173
  238.0 8.0 %fusion.pull_ref = f32[8,2,72,768]{3,2,1,0:T(8,128)} fusion(bf16[8,2,72,2048]{3,2,1,0:T(8,128)(2,1)} %bitcast.19, bf16[1,768,2048]{2,1,0:T(8,128)(2,1)S(1)} %copy-done), kind=kOutput, calls=%fused_computation.1 | convolution fusion | flops 3623878656 | bytes 11403264 | tf_op jit(solution)/shard_map/dot_general | solution.py:28
  246.0 12.4 %shard_map.282 = (bf16[576,768]{1,0:T(8,128)(2,1)}, bf16[576,768]{1,0:T(8,128)(2,1)}, bf16[576,768]{1,0:T(8,128)(2,1)}, bf16[576,2176]{1,0:T(8,128)(2,1)}) custom-call(s32[1]{0:T(128)} %bitcast.10.who_ref, bf16[576,2176]{1,0:T(8,128)(2,1)} %bitcast.14.refs_5_.x_ref, bf16[2048,768]{1,0:T(8,128)(2,1)} %bitcast.130, bf16[2048,768]{1,0:T(8,128)(2,1)} %bitcast.132, ...), custom_call_target="tpu_custom_call" | custom-call | flops 7247757312 | bytes 20000000 | tf_op jit(solution)/shard_map/pallas_call | solution.py:818
  258.5 10.0 %all-to-all-done.2 = bf16[8,72,2176]{2,1,0:T(8,128)(2,1)} async-done(((bf16[8,72,2176]{2,1,0:T(8,128)(2,1)}), bf16[8,72,2176]{2,1,0:T(8,128)(2,1)}, u32[]{:S(2)}, u32[]{:S(2)}) %all-to-all-start.2) | async-done | bytes 2506784 | tf_op jit(solution)/shard_map/all_to_all | solution.py:1306
  268.5 4.8 all-to-all-start.6
  273.3 12.5 %shard_map.281 = (bf16[576,768]{1,0:T(8,128)(2,1)}, bf16[576,768]{1,0:T(8,128)(2,1)}, bf16[576,768]{1,0:T(8,128)(2,1)}, bf16[576,2176]{1,0:T(8,128)(2,1)}) custom-call(s32[1]{0:T(128)} %bitcast.10.who_ref, bf16[576,2176]{1,0:T(8,128)(2,1)} %bitcast.16.x_ref, bf16[2048,768]{1,0:T(8,128)(2,1)} %bitcast.131, bf16[2048,768]{1,0:T(8,128)(2,1)} %bitcast.133, ...), custom_call_target="tpu_custom_call" | custom-call | flops 7247757312 | bytes 20000000 | tf_op jit(solution)/shard_map/pallas_call | solution.py:818
  285.8 18.0 %all-to-all-done.6 = bf16[8,72,2176]{2,1,0:T(8,128)(2,1)} async-done(((bf16[8,72,2176]{2,1,0:T(8,128)(2,1)}), bf16[8,72,2176]{2,1,0:T(8,128)(2,1)}, u32[]{:S(2)}, u32[]{:S(2)}) %all-to-all-start.6) | async-done | bytes 2506784 | tf_op jit(solution)/shard_map/all_to_all | solution.py:1306
  312.2 4.5 shard_map.285.rest_0_
  316.7 7.8 %fusion.13.rest_1_ = f32[2048,768]{1,0:T(8,128)} fusion(bf16[576,2048]{1,0:T(8,128)(2,1)S(1)} %slice.50, bf16[576,2048]{1,0:T(8,128)(2,1)S(1)} %slice.49, bf16[576,768]{1,0:T(8,128)(2,1)} %get-tuple-element.86, bf16[576,768]{1,0:T(8,128)(2,1)} %get-tuple-element.85), kind=kOutput, calls=%fused_computation.10 | convolution fusion | flops 3636854784 | bytes 12779520 | tf_op jit(solution)/shard_map/dot_general | solution.py:32
  324.5 6.4 fusion.12.rest_2_
  330.8 7.9 %all-to-all-done.5 = bf16[8,72,2176]{2,1,0:T(8,128)(2,1)} async-done(((bf16[8,72,2176]{2,1,0:T(8,128)(2,1)}), bf16[8,72,2176]{2,1,0:T(8,128)(2,1)}, u32[]{:S(2)}, u32[]{:S(2)}) %all-to-all-start.5) | async-done | bytes 2506784 | tf_op jit(solution)/shard_map/all_to_all | solution.py:1306
  338.7 4.5 shard_map.286
  343.2 4.6 fusion.6
  355.3 6.3 fusion.20.refs_8_
  361.6 19.5 %all-to-all-done.4 = bf16[8,72,2048]{2,1,0:T(8,128)(2,1)} async-done(((bf16[8,72,2048]{2,1,0:T(8,128)(2,1)}), bf16[8,72,2048]{2,1,0:T(8,128)(2,1)}, u32[]{:S(2)}, u32[]{:S(2)}) %all-to-all-start.4) | async-done | bytes 2359328 | tf_op jit(solution)/shard_map/all_to_all | solution.py:1306
  381.1 5.3 reduce-scatter.9.cloned.1.call-done.refs_0_
  390.7 4.6 fusion.9
  404.2 24.5 %all-to-all-done.3 = bf16[8,72,2048]{2,1,0:T(8,128)(2,1)} async-done(((bf16[8,72,2048]{2,1,0:T(8,128)(2,1)}), bf16[8,72,2048]{2,1,0:T(8,128)(2,1)}, u32[]{:S(2)}, u32[]{:S(2)}) %all-to-all-start.3) | async-done | bytes 2359328 | tf_op jit(solution)/shard_map/all_to_all | solution.py:1306
  436.2 6.8 %shard_map.289 = (bf16[512,2048]{1,0:T(8,128)(2,1)}, bf16[512,2048]{1,0:T(8,128)(2,1)}) custom-call(s32[1]{0:T(128)} %bitcast.27.d_ref, bf16[512,1024]{1,0:T(8,128)(2,1)} %get-tuple-element.70.a_ref.o_ref, bf16[512,2048]{1,0:T(8,128)(2,1)} %all-gather.5.cloned.1.call-done.rows_ref.b_ref, bf16[512,2048]{1,0:T(8,128)(2,1)} %shard_map.284.rest_0_), custom_call_target="tpu_custom_call" | custom-call | flops 2147483648 | bytes 6000000 | tf_op jit(solution)/shard_map/pallas_call | solution.py:477
  443.0 7.8 %shard_map.288 = (bf16[2,8,256,128]{3,2,1,0:T(8,128)(2,1)}, bf16[2,8,128,256]{3,2,1,0:T(8,128)(2,1)}, f32[2,8,8,256]{3,2,1,0:T(8,128)}) custom-call(bf16[512,2048]{1,0:T(8,128)(2,1)} %all-gather.5.cloned.1.call-done.rows_ref.b_ref, bf16[1024,2048]{1,0:T(8,128)(2,1)} %w_ref.3, bf16[512,1024]{1,0:T(8,128)(2,1)} %get-tuple-element.70.a_ref.o_ref, ...), custom_call_target="tpu_custom_call" | custom-call | flops 2147483648 | bytes 12000000 | tf_op jit(solution)/shard_map/pallas_call | solution.py:255
  454.2 4.7 all-to-all-start.7
  458.9 25.7 %shard_map.291 = (f32[2048,256]{1,0:T(8,128)}, bf16[512,1024]{1,0:T(8,128)(2,1)}, f32[1,128]{1,0:T(1,128)}) custom-call(s32[2]{0:T(128)} %get-tuple-element.123.qpos_ref, s32[8]{0:T(128)} %select_reduce_fusion.kidx_ref, bf16[2,8,256,128]{3,2,1,0:T(8,128)(2,1)} %get-tuple-element.68.q_ref, bf16[2,8,128,256]{3,2,1,0:T(8,128)(2,1)} %get-tuple-element.82.qt_ref, ...), custom_call_target="tpu_custom_call" | custom-call | flops 16106127360 | bytes 12000000 | tf_op jit(solution)/shard_map/pallas_call | solution.py:357
  487.3 6.6 %all-to-all-start.8 = ((bf16[4,512,256]{2,1,0:T(8,128)(2,1)}), bf16[4,512,256]{2,1,0:T(8,128)(2,1)}, u32[]{:S(2)}, u32[]{:S(2)}) async-start(bf16[4,512,256]{2,1,0:T(8,128)(2,1)} %bitcast.106), calls=%async_computation.11 | async-start | bytes 2097152 | tf_op jit(solution)/shard_map/all_to_all | solution.py:1086
  496.6 6.7 %shard_map.293 = (bf16[1024,1024]{1,0:T(8,128)(2,1)}, bf16[1024,1024]{1,0:T(8,128)(2,1)}) custom-call(s32[1]{0:T(128)} %bitcast.27.d_ref, bf16[512,2048]{1,0:T(8,128)(2,1)} %get-tuple-element.67.x_ref.a_ref.rows_ref, bf16[512,1024]{1,0:T(8,128)(2,1)} %get-tuple-element.98.b_ref.q_ref, bf16[128,2048]{1,0:T(8,128)(2,1)} %shard_map.292.rest_0_.refs_0_), custom_call_target="tpu_custom_call" | custom-call | flops 2147483648 | bytes 6000000 | tf_op jit(solution)/shard_map/pallas_call | solution.py:477
  503.3 5.5 all-to-all-done.8.parts_ref
  511.4 7.3 %shard_map.295 = (bf16[512,2048]{1,0:T(8,128)(2,1)}, f32[1,2048]{1,0:T(1,128)}) custom-call(bf16[512,1024]{1,0:T(8,128)(2,1)} %get-tuple-element.98.b_ref.q_ref, bf16[512,256]{1,0:T(8,128)(2,1)} %get-tuple-element.102.kv_ref.b_ref, bf16[2048,1024]{1,0:T(8,128)(2,1)} %wq_ref.1, bf16[2048,256]{1,0:T(8,128)(2,1)} %constant_dynamic-update-slice_fusion.refs_7_.wkv_ref, ...), custom_call_target="tpu_custom_call" | custom-call | flops 2684354560 | bytes 12000000 | tf_op jit(solution)/shard_map/pallas_call | solution.py:971
  518.7 4.5 shard_map.299
  525.4 5.2 shard_map.300
  535.2 12.6 %collective-permute-done.16.refs_1_.refs_3_ = bf16[128,2048]{1,0:T(8,128)(2,1)} collective-permute-done((bf16[128,2048]{1,0:T(8,128)(2,1)}, bf16[128,2048]{1,0:T(8,128)(2,1)}, u32[]{:S(2)}, u32[]{:S(2)}) %collective-permute-start.16) | collective-permute-done | bytes 524320 | tf_op jit(solution)/shard_map/ppermute | solution.py:1095
  547.8 11.5 %collective-permute-done.17.refs_2_.refs_4_ = bf16[128,2048]{1,0:T(8,128)(2,1)} collective-permute-done((bf16[128,2048]{1,0:T(8,128)(2,1)}, bf16[128,2048]{1,0:T(8,128)(2,1)}, u32[]{:S(2)}, u32[]{:S(2)}) %collective-permute-start.17) | collective-permute-done | bytes 524320 | tf_op jit(solution)/shard_map/ppermute | solution.py:1095
  574.7 4.7 all-to-all-done.9
  589.6 8.5 %collective-permute-done.27.refs_1_ = bf16[256,1280]{1,0:T(8,128)(2,1)} collective-permute-done((bf16[256,1280]{1,0:T(8,128)(2,1)}, bf16[256,1280]{1,0:T(8,128)(2,1)}, u32[]{:S(2)}, u32[]{:S(2)}) %collective-permute-start.27) | collective-permute-done | bytes 655392 | tf_op jit(solution)/shard_map/ppermute | solution.py:1095
  600.7 7.4 %shard_map.298 = f32[1024,2048]{1,0:T(8,128)} custom-call(s32[8]{0:T(128)} %stack.62.at_ref, bf16[128,2048]{1,0:T(8,128)(2,1)} %shard_map.292.rest_0_.refs_0_, bf16[128,2048]{1,0:T(8,128)(2,1)} %collective-permute-done.16.refs_1_.refs_3_, bf16[128,2048]{1,0:T(8,128)(2,1)} %collective-permute-done.17.refs_2_.refs_4_, ...), custom_call_target="tpu_custom_call" | custom-call | flops 262144 | bytes 12582912 | tf_op jit(solution)/shard_map/pallas_call | solution.py:1061
  625.4 8.2 %shard_map.303 = (f32[2048,1024]{1,0:T(8,128)}, f32[2048,128]{1,0:T(8,128)}, f32[2048,128]{1,0:T(8,128)}) custom-call(s32[8]{0:T(128)} %stack.71.at_ref, bf16[256,1280]{1,0:T(8,128)(2,1)} %shard_map.302.refs_0_, bf16[256,1280]{1,0:T(8,128)(2,1)} %collective-permute-done.27.refs_1_, bf16[256,1280]{1,0:T(8,128)(2,1)} %collective-permute-done.28.refs_2_, ...), custom_call_target="tpu_custom_call" | custom-call | flops 327680 | bytes 15728640 | tf_op jit(solution)/shard_map/pallas_call | solution.py:1061
  (167 shorter events, 163.7 us)
Async XLA Ops:
  7.2 105.1 %all-gather.3.cloned.1.call-start = ((), (), s32[]{:S(2)}) async-start(), calls=%async_computation.15 | async-start | bytes 2785280 | tf_op jit(solution)/shard_map/all_gather | solution.py:1289
  10.7 16.4 %collective-permute-start = (bf16[128,2048]{1,0:T(8,128)(2,1)}, bf16[128,2048]{1,0:T(8,128)(2,1)}, u32[]{:S(2)}, u32[]{:S(2)}) collective-permute-start(bf16[128,2048]{1,0:T(8,128)(2,1)} %fusion.26.refs_3_), channel_id=1, source_target_pairs={{0,1},{1,2},{2,3},{4,5},{5,6},{6,7},{8,9},{9,10},{10,11},{12,13},{... | collective-permute-start | bytes 1572872 | tf_op jit(solution)/shard_map/ppermute | solution.py:1170
  16.4 15.6 %collective-permute-start.3 = (bf16[128,2048]{1,0:T(8,128)(2,1)}, bf16[128,2048]{1,0:T(8,128)(2,1)}, u32[]{:S(2)}, u32[]{:S(2)}) collective-permute-start(bf16[128,2048]{1,0:T(8,128)(2,1)} %fusion.26.refs_3_), channel_id=1, source_target_pairs={{1,0},{2,1},{3,2},{5,4},{6,5},{7,6},{9,8},{10,9},{11,10},{13,12},{... | collective-permute-start | bytes 1572872 | tf_op jit(solution)/shard_map/ppermute | solution.py:1173
  27.1 9.4 %collective-permute-start.1 = (bf16[128,2048]{1,0:T(8,128)(2,1)}, bf16[128,2048]{1,0:T(8,128)(2,1)}, u32[]{:S(2)}, u32[]{:S(2)}) collective-permute-start(bf16[128,2048]{1,0:T(8,128)(2,1)} %collective-permute-done.refs_2_), channel_id=1, source_target_pairs={{1,2},{2,3},{5,6},{6,7},{9,10},{10,11},{13,14},{14,15},{17,18},{18... | collective-permute-start | bytes 1572872 | tf_op jit(solution)/shard_map/ppermute | solution.py:1170
  32.0 14.8 %collective-permute-start.4 = (bf16[128,2048]{1,0:T(8,128)(2,1)}, bf16[128,2048]{1,0:T(8,128)(2,1)}, u32[]{:S(2)}, u32[]{:S(2)}) collective-permute-start(bf16[128,2048]{1,0:T(8,128)(2,1)} %collective-permute-done.3.refs_4_), channel_id=1, source_target_pairs={{1,0},{2,1},{5,4},{6,5},{9,8},{10,9},{13,12},{14,13},{17,16},{18,1... | collective-permute-start | bytes 1572872 | tf_op jit(solution)/shard_map/ppermute | solution.py:1173
  36.5 16.0 %collective-permute-start.2 = (bf16[128,2048]{1,0:T(8,128)(2,1)}, bf16[128,2048]{1,0:T(8,128)(2,1)}, u32[]{:S(2)}, u32[]{:S(2)}) collective-permute-start(bf16[128,2048]{1,0:T(8,128)(2,1)} %collective-permute-done.1.refs_1_), channel_id=1, source_target_pairs={{2,3},{6,7},{10,11},{14,15},{18,19},{22,23},{26,27},{30,31}} | collective-permute-start | bytes 1572872 | tf_op jit(solution)/shard_map/ppermute | solution.py:1170
  46.8 13.9 %collective-permute-start.5 = (bf16[128,2048]{1,0:T(8,128)(2,1)}, bf16[128,2048]{1,0:T(8,128)(2,1)}, u32[]{:S(2)}, u32[]{:S(2)}) collective-permute-start(bf16[128,2048]{1,0:T(8,128)(2,1)} %collective-permute-done.4.refs_5_), channel_id=1, source_target_pairs={{1,0},{5,4},{9,8},{13,12},{17,16},{21,20},{25,24},{29,28}} | collective-permute-start | bytes 1572872 | tf_op jit(solution)/shard_map/ppermute | solution.py:1173
  65.6 95.6 %reduce-scatter.5.cloned.1.call-start = ((), (), s32[]{:S(2)}) async-start(), calls=%async_computation.16 | async-start | bytes 2621440 | tf_op jit(solution)/shard_map/reduce_scatter | solution.py:1312
  66.8 13.8 %collective-permute-start.6 = (bf16[512,256]{0,1:T(8,128)(2,1)S(1)}, bf16[512,256]{0,1:T(8,128)(2,1)S(1)}, u32[]{:S(2)}, u32[]{:S(2)}) collective-permute-start(bf16[512,256]{0,1:T(8,128)(2,1)S(1)} %copy.55), channel_id=1, source_target_pairs={{0,12},{4,8},{8,4},{12,0},{1,13},{5,9},{9,5},{13,1},{2,14},{6,10},... | collective-permute-start | bytes 786440 | tf_op jit(solution)/shard_map/ppermute | solution.py:1182
  69.3 11.3 %collective-permute-start.7 = (bf16[512,256]{0,1:T(8,128)(2,1)S(1)}, bf16[512,256]{0,1:T(8,128)(2,1)S(1)}, u32[]{:S(2)}, u32[]{:S(2)}) collective-permute-start(bf16[512,256]{0,1:T(8,128)(2,1)S(1)} %copy.55), channel_id=1, source_target_pairs={{0,8},{4,12},{8,0},{12,4},{1,9},{5,13},{9,1},{13,5},{2,10},{6,14},... | collective-permute-start | bytes 786440 | tf_op jit(solution)/shard_map/ppermute | solution.py:1182
  69.8 10.8 %collective-permute-start.8 = (bf16[512,256]{0,1:T(8,128)(2,1)S(1)}, bf16[512,256]{0,1:T(8,128)(2,1)S(1)}, u32[]{:S(2)}, u32[]{:S(2)}) collective-permute-start(bf16[512,256]{0,1:T(8,128)(2,1)S(1)} %copy.55), channel_id=1, source_target_pairs={{0,4},{4,0},{8,12},{12,8},{1,5},{5,1},{9,13},{13,9},{2,6},{6,2},{1... | collective-permute-start | bytes 786440 | tf_op jit(solution)/shard_map/ppermute | solution.py:1182
  127.1 59.0 %all-to-all-start = ((bf16[8,144,2048]{2,1,0:T(8,128)(2,1)}), bf16[8,144,2048]{2,1,0:T(8,128)(2,1)}, u32[]{:S(2)}, u32[]{:S(2)}) async-start(bf16[8,144,2048]{2,1,0:T(8,128)(2,1)} %bitcast.104), calls=%async_computation.1 | async-start | bytes 9437184 | tf_op jit(solution)/shard_map/all_to_all | solution.py:1306
  164.2 22.0 %collective-permute-start.9 = (bf16[128,2176]{1,0:T(8,128)(2,1)}, bf16[128,2176]{1,0:T(8,128)(2,1)}, u32[]{:S(2)}, u32[]{:S(2)}) collective-permute-start(bf16[128,2176]{1,0:T(8,128)(2,1)} %get-tuple-element.76.refs_1_), channel_id=1, source_target_pairs={{0,1},{1,2},{2,3},{4,5},{5,6},{6,7},{8,9},{9,10},{10,11},{12,13},{... | collective-permute-start | bytes 1671176 | tf_op jit(solution)/shard_map/ppermute | solution.py:1170
  166.3 19.9 %collective-permute-start.12 = (bf16[128,2176]{1,0:T(8,128)(2,1)}, bf16[128,2176]{1,0:T(8,128)(2,1)}, u32[]{:S(2)}, u32[]{:S(2)}) collective-permute-start(bf16[128,2176]{1,0:T(8,128)(2,1)} %get-tuple-element.76.refs_1_), channel_id=1, source_target_pairs={{1,0},{2,1},{3,2},{5,4},{6,5},{7,6},{9,8},{10,9},{11,10},{13,12},{... | collective-permute-start | bytes 1671176 | tf_op jit(solution)/shard_map/ppermute | solution.py:1173
  190.0 39.3 %all-to-all-start.1 = ((bf16[8,72,2176]{2,1,0:T(8,128)(2,1)}), bf16[8,72,2176]{2,1,0:T(8,128)(2,1)}, u32[]{:S(2)}, u32[]{:S(2)}) async-start(bf16[8,72,2176]{2,1,0:T(8,128)(2,1)} %bitcast.96), calls=%async_computation.2 | async-start | bytes 5013504 | tf_op jit(solution)/shard_map/all_to_all | solution.py:1306
  195.1 18.1 %collective-permute-start.13 = (bf16[128,2176]{1,0:T(8,128)(2,1)}, bf16[128,2176]{1,0:T(8,128)(2,1)S(1)}, u32[]{:S(2)}, u32[]{:S(2)}) collective-permute-start(bf16[128,2176]{1,0:T(8,128)(2,1)} %collective-permute-done.12.refs_2_), channel_id=1, source_target_pairs={{1,0},{2,1},{5,4},{6,5},{9,8},{10,9},{13,12},{14,13},{17,16},{18,1... | collective-permute-start | bytes 1671176 | tf_op jit(solution)/shard_map/ppermute | solution.py:1173
  197.2 17.2 %collective-permute-start.11 = (bf16[128,2176]{1,0:T(8,128)(2,1)S(1)}, bf16[128,2176]{1,0:T(8,128)(2,1)S(1)}, u32[]{:S(2)}, u32[]{:S(2)}) collective-permute-start(bf16[128,2176]{1,0:T(8,128)(2,1)S(1)} %collective-permute-done.10.refs_1_), channel_id=1, source_target_pairs={{2,3},{6,7},{10,11},{14,15},{18,19},{22,23},{26,27},{30,31}} | collective-permute-start | bytes 1671176 | tf_op jit(solution)/shard_map/ppermute | solution.py:1170
  213.2 16.2 %collective-permute-start.14 = (bf16[128,2176]{1,0:T(8,128)(2,1)S(1)}, bf16[128,2176]{1,0:T(8,128)(2,1)}, u32[]{:S(2)}, u32[]{:S(2)}) collective-permute-start(bf16[128,2176]{1,0:T(8,128)(2,1)S(1)} %collective-permute-done.13.refs_3_), channel_id=1, source_target_pairs={{1,0},{5,4},{9,8},{13,12},{17,16},{21,20},{25,24},{29,28}} | collective-permute-start | bytes 1671176 | tf_op jit(solution)/shard_map/ppermute | solution.py:1173
  233.6 34.9 %all-to-all-start.2 = ((bf16[8,72,2176]{2,1,0:T(8,128)(2,1)}), bf16[8,72,2176]{2,1,0:T(8,128)(2,1)}, u32[]{:S(2)}, u32[]{:S(2)}) async-start(bf16[8,72,2176]{2,1,0:T(8,128)(2,1)} %bitcast.97), calls=%async_computation.3 | async-start | bytes 5013504 | tf_op jit(solution)/shard_map/all_to_all | solution.py:1306
  268.5 35.3 %all-to-all-start.6 = ((bf16[8,72,2176]{2,1,0:T(8,128)(2,1)}), bf16[8,72,2176]{2,1,0:T(8,128)(2,1)}, u32[]{:S(2)}, u32[]{:S(2)}) async-start(bf16[8,72,2176]{2,1,0:T(8,128)(2,1)} %bitcast.110), calls=%async_computation.8 | async-start | bytes 5013504 | tf_op jit(solution)/shard_map/all_to_all | solution.py:1306
  303.8 34.9 %all-to-all-start.5 = ((bf16[8,72,2176]{2,1,0:T(8,128)(2,1)}), bf16[8,72,2176]{2,1,0:T(8,128)(2,1)}, u32[]{:S(2)}, u32[]{:S(2)}) async-start(bf16[8,72,2176]{2,1,0:T(8,128)(2,1)} %bitcast.109), calls=%async_computation.7 | async-start | bytes 5013504 | tf_op jit(solution)/shard_map/all_to_all | solution.py:1306
  308.2 78.2 %reduce-scatter.9.cloned.1.call-start = ((), (), s32[]{:S(2)}) async-start(), calls=%async_computation.18 | async-start | bytes 2785280 | tf_op jit(solution)/shard_map/reduce_scatter | solution.py:1344
  347.8 33.3 %all-to-all-start.4 = ((bf16[8,72,2048]{2,1,0:T(8,128)(2,1)}), bf16[8,72,2048]{2,1,0:T(8,128)(2,1)}, u32[]{:S(2)}, u32[]{:S(2)}) async-start(bf16[8,72,2048]{2,1,0:T(8,128)(2,1)} %bitcast.111), calls=%async_computation.5 | async-start | bytes 4718592 | tf_op jit(solution)/shard_map/all_to_all | solution.py:1306
  352.2 84.0 %all-gather.5.cloned.1.call-start = ((), (), s32[]{:S(2)}) async-start(), calls=%async_computation.19 | async-start | bytes 2621440 | tf_op jit(solution)/shard_map/all_gather | solution.py:1362
  395.3 33.3 %all-to-all-start.3 = ((bf16[8,72,2048]{2,1,0:T(8,128)(2,1)}), bf16[8,72,2048]{2,1,0:T(8,128)(2,1)}, u32[]{:S(2)}, u32[]{:S(2)}) async-start(bf16[8,72,2048]{2,1,0:T(8,128)(2,1)} %bitcast.112), calls=%async_computation.4 | async-start | bytes 4718592 | tf_op jit(solution)/shard_map/all_to_all | solution.py:1306
  399.7 172.3 %reduce-scatter.7.cloned.1.call-start = ((), (), s32[]{:S(2)}) async-start(), calls=%async_computation.17 | async-start | bytes 2621440 | tf_op jit(solution)/shard_map/reduce_scatter | solution.py:1367
  443.0 7.8 %collective-permute-start.15 = (bf16[512,2048]{1,0:T(8,128)(2,1)}, bf16[512,2048]{1,0:T(8,128)(2,1)}, u32[]{:S(2)}, u32[]{:S(2)}) collective-permute-start(bf16[512,2048]{1,0:T(8,128)(2,1)} %get-tuple-element.97), channel_id=1, source_target_pairs={{0,16},{16,0},{1,17},{17,1},{2,18},{18,2},{3,19},{19,3},{4,20},{20... | collective-permute-start | bytes 6291464 | tf_op jit(solution)/shard_map/ppermute | solution.py:1077
  454.2 33.1 %all-to-all-start.7 = ((bf16[4,128,2048]{2,1,0:T(8,128)(2,1)}), bf16[4,128,2048]{2,1,0:T(8,128)(2,1)}, u32[]{:S(2)}, u32[]{:S(2)}) async-start(bf16[4,128,2048]{2,1,0:T(8,128)(2,1)} %bitcast.98), calls=%async_computation.10 | async-start | bytes 4194304 | tf_op jit(solution)/shard_map/all_to_all | solution.py:1086
  487.3 21.6 %all-to-all-start.8 = ((bf16[4,512,256]{2,1,0:T(8,128)(2,1)}), bf16[4,512,256]{2,1,0:T(8,128)(2,1)}, u32[]{:S(2)}, u32[]{:S(2)}) async-start(bf16[4,512,256]{2,1,0:T(8,128)(2,1)} %bitcast.106), calls=%async_computation.11 | async-start | bytes 2097152 | tf_op jit(solution)/shard_map/all_to_all | solution.py:1086
  493.9 115.4 %reduce-scatter.11.cloned.1.call-start = ((), (), s32[]{:S(2)}) async-start(), calls=%async_computation.20 | async-start | bytes 2621440 | tf_op jit(solution)/shard_map/reduce_scatter | solution.py:1428
  503.3 22.1 %collective-permute-start.23 = (bf16[1024,1024]{1,0:T(8,128)(2,1)}, bf16[1024,1024]{1,0:T(8,128)(2,1)}, u32[]{:S(2)}, u32[]{:S(2)}) collective-permute-start(bf16[1024,1024]{1,0:T(8,128)(2,1)} %get-tuple-element.110), channel_id=1, source_target_pairs={{0,16},{16,0},{1,17},{17,1},{2,18},{18,2},{3,19},{19,3},{4,20},{20... | collective-permute-start | bytes 6291464 | tf_op jit(solution)/shard_map/ppermute | solution.py:1077
  530.6 28.7 %collective-permute-start.25 = (bf16[512,1280]{1,0:T(8,128)(2,1)}, bf16[512,1280]{1,0:T(8,128)(2,1)}, u32[]{:S(2)}, u32[]{:S(2)}) collective-permute-start(bf16[512,1280]{1,0:T(8,128)(2,1)} %get-tuple-element.114), channel_id=1, source_target_pairs={{0,4},{4,0},{8,12},{12,8},{16,24},{20,28},{24,16},{28,20},{1,5},{5... | collective-permute-start | bytes 3932168 | tf_op jit(solution)/shard_map/ppermute | solution.py:1095
  532.6 15.2 %collective-permute-start.16 = (bf16[128,2048]{1,0:T(8,128)(2,1)}, bf16[128,2048]{1,0:T(8,128)(2,1)}, u32[]{:S(2)}, u32[]{:S(2)}) collective-permute-start(bf16[128,2048]{1,0:T(8,128)(2,1)} %shard_map.292.rest_0_.refs_0_), channel_id=1, source_target_pairs={{0,8},{4,12},{8,0},{12,4},{16,20},{20,16},{24,28},{28,24},{1,9},{5... | collective-permute-start | bytes 1572872 | tf_op jit(solution)/shard_map/ppermute | solution.py:1095
  532.6 26.7 %collective-permute-start.17 = (bf16[128,2048]{1,0:T(8,128)(2,1)}, bf16[128,2048]{1,0:T(8,128)(2,1)}, u32[]{:S(2)}, u32[]{:S(2)}) collective-permute-start(bf16[128,2048]{1,0:T(8,128)(2,1)} %shard_map.292.rest_0_.refs_0_), channel_id=1, source_target_pairs={{0,4},{4,0},{8,12},{12,8},{16,24},{20,28},{24,16},{28,20},{1,5},{5... | collective-permute-start | bytes 1572872 | tf_op jit(solution)/shard_map/ppermute | solution.py:1095
  563.4 16.8 %collective-permute-start.26 = (bf16[256,1280]{1,0:T(8,128)(2,1)}, bf16[256,1280]{1,0:T(8,128)(2,1)}, u32[]{:S(2)}, u32[]{:S(2)}) collective-permute-start(bf16[256,1280]{1,0:T(8,128)(2,1)} %get-tuple-element.116), channel_id=1, source_target_pairs={{0,8},{4,12},{8,0},{12,4},{16,20},{20,16},{24,28},{28,24},{1,9},{5... | collective-permute-start | bytes 1966088 | tf_op jit(solution)/shard_map/ppermute | solution.py:1095
  565.4 14.0 %all-to-all-start.9 = ((bf16[32,2,2048]{2,1,0:T(2,128)(2,1)}), bf16[32,2,2048]{2,1,0:T(2,128)(2,1)S(1)}, u32[]{:S(2)}, u32[]{:S(2)}) async-start(bf16[32,2,2048]{2,1,0:T(2,128)(2,1)} %reshape.167), calls=%async_computation.13 | async-start | bytes 524288 | tf_op jit(solution)/shard_map/all_to_all | solution.py:1423
  570.2 14.2 %collective-permute-start.18 = (bf16[128,2048]{1,0:T(8,128)(2,1)}, bf16[128,2048]{1,0:T(8,128)(2,1)}, u32[]{:S(2)}, u32[]{:S(2)}) collective-permute-start(bf16[128,2048]{1,0:T(8,128)(2,1)} %collective-permute-done.16.refs_1_.refs_3_), channel_id=1, source_target_pairs={{0,4},{4,0},{8,12},{12,8},{16,24},{20,28},{24,16},{28,20},{1,5},{5... | collective-permute-start | bytes 1572872 | tf_op jit(solution)/shard_map/ppermute | solution.py:1095
  582.3 15.7 %collective-permute-start.27 = (bf16[256,1280]{1,0:T(8,128)(2,1)}, bf16[256,1280]{1,0:T(8,128)(2,1)}, u32[]{:S(2)}, u32[]{:S(2)}) collective-permute-start(bf16[256,1280]{1,0:T(8,128)(2,1)} %shard_map.302.refs_0_), channel_id=1, source_target_pairs={{0,8},{4,12},{8,0},{12,4},{16,20},{20,16},{24,28},{28,24},{1,9},{5... | collective-permute-start | bytes 1966088 | tf_op jit(solution)/shard_map/ppermute | solution.py:1095
  583.0 4.9 collective-permute-start.19
  583.9 16.8 %collective-permute-start.20 = (bf16[128,2048]{1,0:T(8,128)(2,1)}, bf16[128,2048]{1,0:T(8,128)(2,1)}, u32[]{:S(2)}, u32[]{:S(2)}) collective-permute-start(bf16[128,2048]{1,0:T(8,128)(2,1)} %collective-permute-done.16.refs_1_.refs_3_), channel_id=1, source_target_pairs={{0,16},{16,0},{1,17},{17,1},{2,18},{18,2},{3,19},{19,3},{4,20},{20... | collective-permute-start | bytes 1572872 | tf_op jit(solution)/shard_map/ppermute | solution.py:1077
  583.9 16.8 %collective-permute-start.21 = (bf16[128,2048]{1,0:T(8,128)(2,1)}, bf16[128,2048]{1,0:T(8,128)(2,1)}, u32[]{:S(2)}, u32[]{:S(2)}) collective-permute-start(bf16[128,2048]{1,0:T(8,128)(2,1)} %collective-permute-done.17.refs_2_.refs_4_), channel_id=1, source_target_pairs={{0,16},{16,0},{1,17},{17,1},{2,18},{18,2},{3,19},{19,3},{4,20},{20... | collective-permute-start | bytes 1572872 | tf_op jit(solution)/shard_map/ppermute | solution.py:1077
  584.4 16.2 %collective-permute-start.22 = (bf16[128,2048]{1,0:T(8,128)(2,1)}, bf16[128,2048]{1,0:T(8,128)(2,1)}, u32[]{:S(2)}, u32[]{:S(2)}) collective-permute-start(bf16[128,2048]{1,0:T(8,128)(2,1)} %collective-permute-done.18.refs_3_), channel_id=1, source_target_pairs={{0,16},{16,0},{1,17},{17,1},{2,18},{18,2},{3,19},{19,3},{4,20},{20... | collective-permute-start | bytes 1572872 | tf_op jit(solution)/shard_map/ppermute | solution.py:1077
  585.3 29.5 %all-to-all-start.10 = ((bf16[32,2,2048]{2,1,0:T(2,128)(2,1)}), bf16[32,2,2048]{2,1,0:T(2,128)(2,1)S(1)}, u32[]{:S(2)}, u32[]{:S(2)}) async-start(bf16[32,2,2048]{2,1,0:T(2,128)(2,1)} %broadcast_in_dim.85), calls=%async_computation.14 | async-start | bytes 524288 | tf_op jit(solution)/shard_map/all_to_all | solution.py:1423
  587.9 32.4 %collective-permute-start.28 = (bf16[256,1280]{1,0:T(8,128)(2,1)}, bf16[256,1280]{1,0:T(8,128)(2,1)}, u32[]{:S(2)}, u32[]{:S(2)}) collective-permute-start(bf16[256,1280]{1,0:T(8,128)(2,1)} %shard_map.302.refs_0_), channel_id=1, source_target_pairs={{0,4},{4,0},{8,12},{12,8},{16,24},{20,28},{24,16},{28,20},{1,5},{5... | collective-permute-start | bytes 1966088 | tf_op jit(solution)/shard_map/ppermute | solution.py:1095
  598.0 22.2 %collective-permute-start.29 = (bf16[256,1280]{1,0:T(8,128)(2,1)}, bf16[256,1280]{1,0:T(8,128)(2,1)}, u32[]{:S(2)}, u32[]{:S(2)}) collective-permute-start(bf16[256,1280]{1,0:T(8,128)(2,1)} %collective-permute-done.27.refs_1_), channel_id=1, source_target_pairs={{0,4},{4,0},{8,12},{12,8},{16,24},{20,28},{24,16},{28,20},{1,5},{5... | collective-permute-start | bytes 1966088 | tf_op jit(solution)/shard_map/ppermute | solution.py:1095
  609.3 14.2 %collective-permute-start.30 = (bf16[256,1280]{1,0:T(8,128)(2,1)}, bf16[256,1280]{1,0:T(8,128)(2,1)}, u32[]{:S(2)}, u32[]{:S(2)}) collective-permute-start(bf16[256,1280]{1,0:T(8,128)(2,1)} %shard_map.302.refs_0_), channel_id=1, source_target_pairs={{0,16},{16,0},{1,17},{17,1},{2,18},{18,2},{3,19},{19,3},{4,20},{20... | collective-permute-start | bytes 1966088 | tf_op jit(solution)/shard_map/ppermute | solution.py:1077
  619.7 3.8 collective-permute-start.31
  620.2 3.8 collective-permute-start.33
  (17 other events, 308.6 us)
Sparse Core Ops, SparseCore 0:
  65.8 46.5 all-gather.2
  118.5 42.7 reduce-scatter.4
  343.4 43.0 reduce-scatter.8
  390.9 45.3 all-gather.4
  443.1 42.7 reduce-scatter.6
  518.8 42.1 reduce-scatter.10
